TPU v7x, 512 devices: a whole 4x8x8 slice. The times are simulated.
512 devices in a mesh: ctx: 64 (over x, z, core), head: 8 (over y).
Axes of the slice: x: 4, y: 8, z: 8, core: 2. Of those that a mesh axis runs over, the one named last changes fastest.
Arguments:
- xin: bfloat16 [16384, 4096], P('ctx', 'head'), may hold values from -6 to 6
- zin: bfloat16 [16384, 4096], P('ctx', 'head'), may hold values from -6 to 6
- bmat: bfloat16 [16384, 128], P('ctx'), may hold values from -6 to 6
- cmat: bfloat16 [16384, 128], P('ctx'), may hold values from -6 to 6
- ldec: float32 [64, 16384], P('head', 'ctx'), may hold values from -1 to 0, as said below
- dskip: float32 [64], P('head'), may hold values from 0.5 to 2
- gain: float32 [4096], P('head'), may hold values from 0.1 to 1.9
- w_out: bfloat16 [2048, 4096], P('ctx', 'head'), may hold values from -0.09375 to 0.09375
- dout: bfloat16 [16384, 2048], P('ctx', 'head'), may hold values from -16 to 16
Outputs:
- grad_x: bfloat16 [16384, 4096], P('ctx', 'head')
- grad_z: bfloat16 [16384, 4096], P('ctx', 'head')
- grad_b: float32 [16384, 128], P('ctx')
- grad_c: float32 [16384, 128], P('ctx')
- grad_w: float32 [2048, 4096], P('ctx', 'head')
- grad_gain: float32 [4096], P('head')
- grad_skip: float32 [64], P('head')
Inputs may be any that keep to these rules, and one draw needn't show every extreme that they name: `ldec`: every entry is at most zero.
All inputs are finite; a program needn't handle non-finite values.
Results may differ from a plain program's by a relative error of at most 0.0015.
Values may be sent and summed in bfloat16 or wider, within the bound.
A program may use at most 128 MiB of HBM per device.

v0:
```python
import jax
import jax.numpy as jnp
from jax import lax
from jax.sharding import PartitionSpec as P

HDIM = 64


HIGH = lax.Precision.HIGHEST
EPSILON = 1e-05


def carried_in(value, axis, join, neutral, backward):
    count, mine = (lax.axis_size(axis), lax.axis_index(axis))
    pieces = jax.tree.map(lambda part: lax.all_gather(part, axis), value)
    if backward:
        pieces = jax.tree.map(lambda part: part[::-1], pieces)
        mine = count - 1 - mine
    total = jax.tree.map(
        lambda part, zero: jnp.full_like(part, 0) + jnp.asarray(zero, part.dtype), value, neutral
    )

    def turn(position, total):
        longer = join(total, jax.tree.map(lambda part: part[position], pieces))
        return jax.tree.map(lambda new, old: jnp.where(position < mine, new, old), longer, total)

    return lax.fori_loop(0, count - 1, turn, total)


def combine(earlier_tokens, later):
    return (earlier_tokens[0] * later[0], later[0][:, None, None] * earlier_tokens[1] + later[1])


def per_device(xin, zin, bmat, cmat, ldec, dskip, gain, w_out, dout):
    heads_here, tokens_here = ldec.shape
    values_x = xin.astype(jnp.float32).reshape(tokens_here, heads_here, HDIM)
    values_b = bmat.astype(jnp.float32)
    values_c = cmat.astype(jnp.float32)
    cot_full = lax.all_gather(dout, "head", axis=1, tiled=True)
    columns = cot_full
    normed_grad = jnp.dot(
        columns,
        lax.all_gather(w_out, "ctx", axis=0, tiled=True),
        preferred_element_type=jnp.float32,
    )
    cumlog = jnp.cumsum(ldec, axis=1)
    positions = jnp.arange(tokens_here)
    causal = positions[:, None] >= positions[None, :]
    gaps = cumlog[:, :, None] - cumlog[:, None, :]
    decays = jnp.where(causal[None], jnp.exp(jnp.where(causal[None], gaps, 0.0)), 0.0)
    scores = jnp.dot(values_c, values_b.T, precision=HIGH)
    kernel = decays * scores[None]
    inner_out = jnp.einsum("hts,shp->thp", kernel, values_x, precision=HIGH)
    tail = jnp.exp(cumlog[:, -1:] - cumlog)
    increasing_order = jnp.exp(cumlog)
    local_state = jnp.einsum("ht,thp,tn->hpn", tail, values_x, values_b, precision=HIGH)
    total_decay = jnp.exp(cumlog[:, -1])
    identity = (jnp.ones_like(total_decay), jnp.zeros_like(local_state))
    _, incoming_hidden = carried_in((total_decay, local_state), "ctx", combine, identity, False)
    carried = (
        jnp.einsum("hpn,tn->thp", incoming_hidden, values_c, precision=HIGH)
        * increasing_order.T[:, :, None]
    )
    mixed = inner_out + carried + dskip[None, :, None] * values_x
    mixed = mixed.reshape(tokens_here, -1)
    values_z = zin.astype(jnp.float32)
    sigmoid_z = jax.nn.sigmoid(values_z)
    gate_act = values_z * sigmoid_z
    gated = mixed * gate_act
    weighted = gain * normed_grad
    features_all = gated.shape[1] * lax.axis_size("head")
    square_total = lax.psum(jnp.sum(gated * gated, axis=1), "head")
    inv_rms = lax.rsqrt(square_total / features_all + EPSILON)[:, None]
    normed = gated * inv_rms * gain
    cot_wide = cot_full.astype(jnp.float32)
    inner_total = lax.psum(jnp.sum(weighted * gated, axis=1), "head")
    gain_part = jnp.sum(normed_grad * gated * inv_rms, axis=0)
    gated_grad = (
        inv_rms * weighted
        - gated * (inv_rms * inv_rms * inv_rms) * (inner_total / features_all)[:, None]
    )
    mixed_grad = gated_grad * gate_act
    grad_z = gated_grad * mixed * sigmoid_z * (1.0 + values_z * (1.0 - sigmoid_z))
    head_grad = mixed_grad.reshape(tokens_here, heads_here, HDIM)
    skip_part = jnp.sum(head_grad * values_x, axis=(0, 2))
    local_grad = jnp.einsum("ht,thp,tn->hpn", increasing_order, head_grad, values_c, precision=HIGH)
    _, grad_in = carried_in((total_decay, local_grad), "ctx", combine, identity, True)
    products = jnp.einsum("thp,shp->hts", head_grad, values_x, precision=HIGH) * decays
    grad_x = jnp.einsum("hts,thp->shp", kernel, head_grad, precision=HIGH)
    grad_x = (
        grad_x + jnp.einsum("hpn,sn->shp", grad_in, values_b, precision=HIGH) * tail.T[:, :, None]
    )
    grad_x = grad_x + dskip[None, :, None] * head_grad
    grad_b = jnp.einsum("hts,tn->sn", products, values_c, precision=HIGH)
    grad_b = grad_b + jnp.einsum("hpn,shp,hs->sn", grad_in, values_x, tail, precision=HIGH)
    grad_c = jnp.einsum("hts,sn->tn", products, values_b, precision=HIGH)
    grad_c = grad_c + jnp.einsum(
        "hpn,thp,ht->tn", incoming_hidden, head_grad, increasing_order, precision=HIGH
    )
    grad_b, grad_c = lax.psum((grad_b, grad_c), "head")
    columns = cot_wide
    grad_w = lax.psum_scatter(
        lax.dot_general(
            columns,
            normed,
            (((0,), (0,)), ((), ())),
            precision=HIGH,
            preferred_element_type=jnp.float32,
        ),
        "ctx",
        scatter_dimension=0,
        tiled=True,
    )
    grad_gain, grad_skip = lax.psum((gain_part, skip_part), "ctx")
    return (
        grad_x.reshape(tokens_here, -1).astype(jnp.bfloat16),
        grad_z.astype(jnp.bfloat16),
        grad_b,
        grad_c,
        grad_w,
        grad_gain,
        grad_skip,
    )


def solution(mesh):
    return jax.shard_map(
        per_device,
        mesh=mesh,
        in_specs=(
            P("ctx", "head"),
            P("ctx", "head"),
            P("ctx", None),
            P("ctx", None),
            P("head", "ctx"),
            P("head"),
            P("head"),
            P("ctx", "head"),
            P("ctx", "head"),
        ),
        out_specs=(
            P("ctx", "head"),
            P("ctx", "head"),
            P("ctx", None),
            P("ctx", None),
            P("ctx", "head"),
            P("head"),
            P("head"),
        ),
        check_vma=False,
    )
```

profile of v0, /device:TPU:1, one launch (start us, length us, event | category | flops | bytes accessed | tf_op | source)
XLA Modules:
  0.0 613.0 jit_solution(8193812396327533917)
XLA Ops:
  7.2 1.3 reduce-window.6
  9.0 1.1 copy.50
  10.1 1.9 fusion.30
  13.7 1.1 copy.51
  14.8 1.3 dynamic-slice
  17.0 132.2 %all-reduce = f32[512]{0:T(512)S(1)} all-reduce(f32[512]{0:T(512)S(1)} %dynamic-update-slice), channel_id=2, replica_groups=mesh['ctx'=64,'head'=8] {'ctx'}, use_global_device_ids=true, to_apply=%add | all-reduce | flops 512 | bytes 4096
  149.5 1.7 fusion.7
  151.2 68.9 %while.28 = (s32[]{:T(128)}, f32[8,64,128]{2,1,0:T(8,128)S(1)}, s32[]{:T(128)}, f32[64,8]{1,0:T(8,128)S(1)}, f32[64,8,64,128]{3,2,1,0:T(8,128)}, /*index=5*/s32[]{:T(128)}, s32[]{:T(128)}) while((s32[]{:T(128)}, f32[8,64,128]{2,1,0:T(8,128)S(1)}, s32[]{:T(128)}, f32[64,8]{1,0:T(8,128)S(1)}, f32[64,8,64,128]{3,2,1,0:T(8,128)}, ...), condition=%wide.region_3.4_spmd.clone, body=%wide.region_2.3_spmd.clone.sunk | while | flops 262148 | bytes 786633 | solution.py:27
  152.4 1.1 fusion.81
  157.8 1.1 fusion.81
  188.5 1.1 fusion.81
  197.2 1.1 fusion.81
  221.4 14.8 %psum.42 = f32[256]{0:T(256)S(1)} all-reduce(f32[256]{0:T(256)S(1)} %multiply_reduce_fusion.4), channel_id=1, replica_groups=mesh['ctx'=64,'head'=8] {'head'}, use_global_device_ids=true, to_apply=%region_5.6 | all-reduce | flops 256 | bytes 2048 | tf_op jit(solution)/shard_map/psum | solution.py:72
  236.2 15.3 %all-gather.10.cloned.1.call-done = bf16[2048,512]{1,0:T(8,128)(2,1)} async-done(((bf16[32,512]{1,0:T(8,128)(2,1)}), bf16[2048,512]{1,0:T(8,128)(2,1)}) %all-gather.10.cloned.1.call-update) | async-done | bytes 2097168 | tf_op jit(solution)/shard_map/all_gather | solution.py:43
  251.5 2.8 multiply_reduce_fusion.2
  254.4 13.4 %psum.43 = f32[256]{0:T(256)S(1)} all-reduce(f32[256]{0:T(256)S(1)} %get-tuple-element.269), channel_id=1, replica_groups=mesh['ctx'=64,'head'=8] {'head'}, use_global_device_ids=true, to_apply=%region_7.8 | all-reduce | flops 256 | bytes 2048 | tf_op jit(solution)/shard_map/psum | solution.py:76
  267.8 1.1 multiply_reduce_fusion.1
  269.2 1.1 fusion.42
  270.5 5.1 convolution_bitcast_fusion
  275.6 5.4 copy.57
  282.2 1.5 multiply_reduce_fusion
  284.7 1.9 fusion.10
  286.7 128.9 %all-reduce.1 = (f32[512]{0:T(512)}, f32[8]{0:T(128)}) all-reduce(f32[512]{0:T(512)S(1)} %get-tuple-element.268, f32[8]{0:T(128)S(1)} %reduce_sum.62), channel_id=1, replica_groups=mesh['ctx'=64,'head'=8] {'ctx'}, use_global_device_ids=true, to_apply=%region_15.16 | all-reduce | flops 520 | bytes 4160 | tf_op jit(solution)/shard_map/psum | solution.py:114
  415.6 12.0 %rev.7 = f32[64,8,64,128]{3,2,1,0:T(8,128)} reverse(f32[64,8,64,128]{3,2,1,0:T(8,128)} %bitcast.98), dimensions={0} | reverse | bytes 33554432 | tf_op jit(solution)/shard_map/rev | solution.py:17
  427.6 69.1 %while.29 = (s32[]{:T(128)}, f32[8,64,128]{2,1,0:T(8,128)S(1)}, s32[]{:T(128)}, f32[64,8]{1,0:T(8,128)S(1)}, f32[64,8,64,128]{3,2,1,0:T(8,128)}, /*index=5*/s32[]{:T(128)}, s32[]{:T(128)}) while((s32[]{:T(128)}, f32[8,64,128]{2,1,0:T(8,128)S(1)}, s32[]{:T(128)}, f32[64,8]{1,0:T(8,128)S(1)}, f32[64,8,64,128]{3,2,1,0:T(8,128)}, ...), condition=%wide.region_9.10_spmd.clone, body=%wide.region_8.9_spmd.clone.sunk | while | flops 262148 | bytes 786633 | solution.py:27
  428.7 1.1 fusion.82
  429.8 1.1 fusion.82
  430.9 1.1 fusion.82
  432.0 1.1 fusion.82
  433.1 1.1 fusion.82
  434.2 1.1 fusion.82
  435.3 1.1 fusion.82
  436.4 1.1 fusion.82
  437.5 1.1 fusion.82
  438.6 1.1 fusion.82
  439.7 1.1 fusion.82
  440.8 1.1 fusion.82
  441.9 1.1 fusion.82
  443.0 1.1 fusion.82
  444.1 1.1 fusion.82
  458.3 1.1 fusion.82
  459.4 1.1 fusion.82
  464.9 1.1 fusion.82
  466.0 1.1 fusion.82
  468.2 1.1 fusion.82
  470.4 1.1 fusion.82
  471.5 1.1 fusion.82
  472.6 1.1 fusion.82
  473.7 1.1 fusion.82
  474.8 1.1 fusion.82
  475.9 1.1 fusion.82
  477.0 1.1 fusion.82
  478.1 1.1 fusion.82
  479.2 1.1 fusion.82
  480.3 1.1 fusion.82
  481.4 1.1 fusion.82
  482.5 1.1 fusion.82
  483.6 1.1 fusion.82
  484.7 1.1 fusion.82
  485.8 1.1 fusion.82
  500.0 24.4 %reduce-scatter.4.cloned.1.call-done = f32[32,512]{1,0:T(8,128)} async-done(((f32[2048,512]{1,0:T(8,128)}), f32[32,512]{1,0:T(8,128)}) %reduce-scatter.4.cloned.1.call-update) | async-done | bytes 65552
  524.4 78.6 %all-reduce.5.cloned.1.call-done = (f32[256,128]{1,0:T(8,128)}, f32[256,128]{1,0:T(8,128)}) async-done(((f32[256,128]{1,0:T(8,128)}, f32[256,128]{1,0:T(8,128)}), (f32[256,128]{1,0:T(8,128)}, f32[256,128]{1,0:T(8,128)})) %all-reduce.5.cloned.1.call-update) | async-done | bytes 262160 | tf_op jit(solution)/shard_map/psum | solution.py:100
  603.0 1.6 copy.74
  604.6 1.6 copy.75
  (268 shorter events, 102.6 us)
Async XLA Ops:
  7.2 142.1 %copy-start = (bf16[256,128]{1,0:T(8,128)(2,1)S(1)}, bf16[256,128]{1,0:T(8,128)(2,1)}, u32[]{:S(2)}) copy-start(bf16[256,128]{1,0:T(8,128)(2,1)} %param.16) | copy-start | bytes 196612
  7.2 142.1 %copy-start.3 = (bf16[256,128]{1,0:T(8,128)(2,1)S(1)}, bf16[256,128]{1,0:T(8,128)(2,1)}, u32[]{:S(2)}) copy-start(bf16[256,128]{1,0:T(8,128)(2,1)} %param.15) | copy-start | bytes 196612
  7.2 144.0 %all-gather.12.cloned.1.call-start = ((), (), s32[]{:S(2)}) async-start(), calls=%async_computation.3 | async-start | bytes 17039360 | tf_op jit(solution)/shard_map/all_gather | solution.py:15
  12.1 224.1 %all-gather.8.cloned.1.call-start = ((), (), s32[]{:S(2)}) async-start(), calls=%async_computation.1 | async-start | bytes 1179648 | tf_op jit(solution)/shard_map/all_gather | solution.py:39
  12.9 238.6 %all-gather.10.cloned.1.call-start = ((), (), s32[]{:S(2)}) async-start(), calls=%async_computation.2 | async-start | bytes 2129920 | tf_op jit(solution)/shard_map/all_gather | solution.py:43
  13.6 402.0 %all-gather.14.cloned.1.call-start = ((), (), s32[]{:S(2)}) async-start(), calls=%async_computation.4 | async-start | bytes 17039360 | tf_op jit(solution)/shard_map/all_gather | solution.py:15
  151.2 69.0 %copy-start.5 = (f32[8]{0:T(128)S(1)}, f32[8]{0:T(128)}, u32[]{:S(2)}) copy-start(f32[8]{0:T(128)} %param.18) | copy-start | bytes 100
  220.2 1.0 copy-start.1
  220.2 31.3 %copy-start.4 = (f32[512]{0:T(512)S(1)}, f32[512]{0:T(512)}, u32[]{:S(2)}) copy-start(f32[512]{0:T(512)} %param.19) | copy-start | bytes 6148
  251.5 16.3 %copy-start.2 = (bf16[256,512]{1,0:T(8,128)(2,1)S(1)}, bf16[256,512]{1,0:T(8,128)(2,1)}, u32[]{:S(2)}) copy-start(bf16[256,512]{1,0:T(8,128)(2,1)} %param.13) | copy-start | bytes 786436
  270.3 254.2 %reduce-scatter.4.cloned.1.call-start = ((), (), s32[]{:S(2)}) async-start(), calls=%async_computation.5 | async-start | bytes 4259840
  286.6 316.4 %all-reduce.5.cloned.1.call-start = ((), (), s32[]{:S(2)}) async-start(), calls=%async_computation.6 | async-start | bytes 524288 | tf_op jit(solution)/shard_map/psum | solution.py:100
Sparse Core Ops, SparseCore 0:
  12.2 112.4 all-gather.11
  126.7 34.7 all-gather.7
  164.8 86.6 all-gather.9
  270.4 104.9 all-gather.13
  380.5 143.8 reduce-scatter.3
  527.4 75.6 all-reduce.4
where the time goes:
time: 622 us; the launch traced here: 613 us
  blocking collectives  289 us (46%)
  other arithmetic  136 us (22%)
  waiting for transfers between devices  120 us (19%)
  local copies, waits for them, and re-layouts  27.5 us (4%)
  matrix products  21 us (3%)
  between operations  15 us (2%)
    select_n x126, other arithmetic, turn(): jnp.where(position < mine, new, old)  133 us
    unnamed x1, blocking collectives  132 us
    psum x1, blocking collectives, per_device(): grad_gain, grad_skip = lax.psum((gain_part, skip_part), 'ctx')  129 us
    psum x1, waiting for transfers between devices, per_device(): grad_b, grad_c = lax.psum((grad_b, grad_c), 'head')  78.6 us
    unnamed x7, waiting for transfers between devices  25.9 us
    all_gather x1, waiting for transfers between devices, per_device(): lax.all_gather(w_out, 'ctx', axis=0, tiled=True)  15.3 us
    psum x1, blocking collectives, per_device(): square_total = lax.psum(jnp.sum(gated * gated, axis=1), 'head')  14.8 us
    psum x1, blocking collectives, per_device(): inner_total = lax.psum(jnp.sum(weighted * gated, axis=1), 'head')  13.4 us
  transfers between devices with their start and end apart: 6, of which 3 were waited for; matrix products, arithmetic and copies ran while one was open for 28% of the time, Pallas kernels for 0%

commit v1 on v0

v1 whole, which is shorter than its diff:
```python
import functools
import jax
import jax.numpy as jnp
from jax import lax
from jax.experimental import pallas as pl
from jax.experimental.pallas import tpu as pltpu
from jax.sharding import PartitionSpec as P

HDIM = 64
HIGH = lax.Precision.HIGHEST
EPSILON = 1e-05
MESH = pl.DeviceIdType.MESH
NX, NZ, NC = 4, 8, 2
VMEM_LIMIT = 48 * 2**20


def remote(src, dst, sent, came, **where):
    return pltpu.make_async_remote_copy(
        src_ref=src, dst_ref=dst, send_sem=sent, recv_sem=came, device_id=where, device_id_type=MESH
    )


def wait_for(ref, sem):
    pltpu.make_async_copy(ref, ref, sem).wait()


def others(axis, act):
    count, mine = lax.axis_size(axis), lax.axis_index(axis)

    def turn(step, carry):
        act(lax.rem(mine + step, count))
        return carry

    lax.fori_loop(1, count, turn, 0)


def greet(*axes):
    barrier = pltpu.get_barrier_semaphore()
    total = 0
    for axis in axes:
        others(
            axis,
            lambda peer: pl.semaphore_signal(
                barrier, inc=1, device_id={axis: peer}, device_id_type=MESH
            ),
        )
        total += lax.axis_size(axis) - 1
    pl.semaphore_wait(barrier, total)


def coordinates():
    mine = lax.axis_index("ctx")
    return mine // (NZ * NC), lax.rem(mine // NC, NZ), lax.rem(mine, NC)


def ctx_of(x, z, core):
    return (x * NZ + z) * NC + core


def scan_send(local, got, sent, came):
    mine = lax.axis_index("ctx")
    rows = got.shape[1]

    def part(index):
        return local.at[pl.ds(pl.multiple_of(index * rows, rows), rows)]

    others("ctx", lambda peer: remote(part(peer), got.at[mine], sent, came, ctx=peer).start())
    pltpu.make_async_copy(part(mine), got.at[mine], came).start()


def scan_turn(got, decays, before, out, sent, came, came_back, backward):
    mine = lax.axis_index("ctx")
    count, rows = got.shape[0], got.shape[1]
    wait_for(got, came)

    def turn(step, total):
        index = count - 1 - step if backward else step
        before[index] = total
        return decays[index] * total + got[index]

    lax.fori_loop(0, count, turn, jnp.zeros(got.shape[1:], jnp.float32))
    home = out.at[pl.ds(pl.multiple_of(mine * rows, rows), rows)]
    others("ctx", lambda peer: remote(before.at[peer], home, sent, came_back, ctx=peer).start())
    pltpu.make_async_copy(before.at[mine], home, came_back).start()


def scan_end(got, out, sent, sent_back, came_back):
    count = got.shape[0]
    wait_for(out, came_back)
    wait_for(got.at[pl.ds(0, count - 1)], sent)
    wait_for(got.at[pl.ds(0, count - 1)], sent_back)


def first_kernel(
    state, decay, w_mine, dout_mine, came_in, decays, w_all, dout_all,
    got, before, state_sems, decay_sems, w_sent, w_z, w_x, w_core, w_own, d_sent, d_came,
):
    greet("ctx", "head")
    mine, row = lax.axis_index("ctx"), lax.axis_index("head")
    count, rows_count = lax.axis_size("ctx"), lax.axis_size("head")
    x, z, core = coordinates()
    slice_rows = got.shape[1]
    heads_per = HDIM // slice_rows
    others(
        "ctx",
        lambda peer: remote(
            decay.at[peer // heads_per], decays.at[mine], decay_sems.at[0], decay_sems.at[1], ctx=peer
        ).start(),
    )
    pltpu.make_async_copy(decay.at[mine // heads_per], decays.at[mine], decay_sems.at[1]).start()
    scan_send(state, got, state_sems.at[0], state_sems.at[1])
    w_home = pltpu.make_async_copy(w_mine, w_all.at[x, z, core], w_own)
    w_home.start()
    for step in range(1, NZ):
        peer = lax.rem(z + step, NZ)
        remote(w_mine, w_all.at[x, z, core], w_sent, w_z.at[step], ctx=ctx_of(x, peer, core)).start()
    right, left = lax.rem(row + 1, rows_count), lax.rem(row + rows_count - 1, rows_count)
    far, near = rows_count // 2, rows_count - 1 - rows_count // 2

    def ring(step):
        if step < far:
            piece = lax.rem(row + rows_count - step, rows_count)
            source = dout_mine if step == 0 else dout_all.at[piece]
            if step:
                wait_for(dout_all.at[piece], d_came.at[0, step])
            remote(source, dout_all.at[piece], d_sent, d_came.at[0, step + 1], head=right).start()
        if step < near:
            piece = lax.rem(row + step, rows_count)
            source = dout_mine if step == 0 else dout_all.at[piece]
            if step:
                wait_for(dout_all.at[piece], d_came.at[1, step])
            remote(source, dout_all.at[piece], d_sent, d_came.at[1, step + 1], head=left).start()

    ring(0)
    for step in range(NX - 1):
        peer = lax.rem(x + step + 1, NX)
        remote(
            w_mine, w_all.at[x, z, core], w_sent, w_x.at[step], ctx=ctx_of(peer, z, core)
        ).start()
    for step in range(1, NZ):
        source = lax.rem(z + NZ - step, NZ)
        wait_for(w_all.at[x, source, core], w_z.at[step])
        for turn in range(NX - 1):
            peer = lax.rem(x + turn + 1, NX)
            remote(
                w_all.at[x, source, core], w_all.at[x, source, core], w_sent, w_x.at[turn],
                ctx=ctx_of(peer, z, core),
            ).start()
    w_home.wait()
    twin = ctx_of(x, z, 1 - core)
    remote(w_all.at[x, :, core], w_all.at[x, :, core], w_sent, w_core.at[0], ctx=twin).start()
    wait_for(decays, decay_sems.at[1])
    scan_turn(
        got, decays, before, came_in, state_sems.at[2], state_sems.at[1], state_sems.at[3], False
    )
    for step in range(1, far):
        ring(step)
    for turn in range(NX - 1):
        source = lax.rem(x + NX - turn - 1, NX)
        wait_for(w_all.at[source, :, core], w_x.at[turn])
        remote(
            w_all.at[source, :, core], w_all.at[source, :, core], w_sent, w_core.at[turn + 1], ctx=twin
        ).start()
    dout_all[row] = dout_mine[...]
    wait_for(dout_all.at[lax.rem(row + rows_count - far, rows_count)], d_came.at[0, far])
    if near:
        wait_for(dout_all.at[lax.rem(row + near, rows_count)], d_came.at[1, near])
    for turn in range(NX):
        source = lax.rem(x + NX - turn, NX)
        wait_for(w_all.at[source, :, 1 - core], w_core.at[turn])
    scan_end(got, came_in, state_sems.at[0], state_sems.at[2], state_sems.at[3])
    wait_for(decays.at[pl.ds(0, count - 1)], decay_sems.at[0])
    wait_for(dout_all.at[pl.ds(0, rows_count - 1)], d_sent)
    for turn in range(NX):
        wait_for(w_all.at[turn, :, 0], w_sent)
    for turn in range(NX - 1):
        wait_for(w_all.at[turn, :, 0], w_sent)
    wait_for(w_all.at[0, pl.ds(0, NZ - 1), 0], w_sent)


def sum_kernel(part, total, got, sent, came):
    greet("head")
    mine, count = lax.axis_index("head"), lax.axis_size("head")
    others("head", lambda peer: remote(part, got.at[mine], sent, came, head=peer).start())
    pltpu.make_async_copy(part, got.at[mine], came).start()
    wait_for(got, came)
    value = got[0]
    for index in range(1, count):
        value = value + got[index]
    total[...] = value
    wait_for(got.at[pl.ds(0, count - 1)], sent)


def shared_kernel(part, total, got, summed, sems):
    greet("head")
    mine, count = lax.axis_index("head"), lax.axis_size("head")
    rows = got.shape[1]

    def at(ref, index):
        return ref.at[pl.ds(pl.multiple_of(index * rows, rows), rows)]

    others(
        "head", lambda peer: remote(at(part, peer), got.at[mine], sems.at[0], sems.at[1], head=peer).start()
    )
    pltpu.make_async_copy(at(part, mine), got.at[mine], sems.at[1]).start()
    wait_for(got, sems.at[1])
    value = got[0]
    for index in range(1, count):
        value = value + got[index]
    summed[...] = value
    others(
        "head", lambda peer: remote(summed, at(total, mine), sems.at[2], sems.at[3], head=peer).start()
    )
    pltpu.make_async_copy(summed, at(total, mine), sems.at[3]).start()
    wait_for(total, sems.at[3])
    wait_for(got.at[pl.ds(0, count - 1)], sems.at[0])
    wait_for(got.at[pl.ds(0, count - 1)], sems.at[2])


PARTS = 2


def second_kernel(
    state, decays, grads, gains, came_in, grad, gain_total,
    got, before, twin_got, mid, x_got, low, z_got, gains_got,
    state_sems, gain_sems, twin_sems, x_sent, x_came, z_sent, z_came,
):
    greet("ctx")
    mine, count = lax.axis_index("ctx"), lax.axis_size("ctx")
    x, z, core = coordinates()
    twin = ctx_of(x, z, 1 - core)
    depth = NZ // PARTS
    order = [lax.rem(x + step, NX) for step in range(1, NX + 1)]
    scan_send(state, got, state_sems.at[0], state_sems.at[1])
    for step in range(NX):
        remote(
            grads.at[order[step], :, 1 - core], twin_got.at[order[step]], twin_sems.at[0, step],
            twin_sems.at[1, step], ctx=twin,
        ).start()
    others(
        "ctx", lambda peer: remote(gains, gains_got.at[mine], gain_sems.at[0], gain_sems.at[1], ctx=peer).start()
    )
    pltpu.make_async_copy(gains, gains_got.at[mine], gain_sems.at[1]).start()
    for step in range(NX):
        wait_for(twin_got.at[order[step]], twin_sems.at[1, step])

        def add(index, carry):
            mid[order[step], index] = (
                grads[order[step], index, core] + twin_got[order[step], index]
            )
            return carry

        lax.fori_loop(0, NZ, add, 0)
        if step < NX - 1:
            for part in range(PARTS):
                block = pl.ds(part * depth, depth)
                remote(
                    mid.at[order[step], block], x_got.at[step, block], x_sent, x_came.at[part, step],
                    ctx=ctx_of(order[step], z, core),
                ).start()
    scan_turn(
        got, decays, before, came_in, state_sems.at[2], state_sems.at[1], state_sems.at[3], True
    )
    for part in range(PARTS):
        block = pl.ds(part * depth, depth)
        for step in range(NX - 1):
            wait_for(x_got.at[step, block], x_came.at[part, step])

        def fold(turn, carry):
            index = lax.rem(z + turn + 1, NZ)

            @pl.when((index >= part * depth) & (index < (part + 1) * depth))
            def _():
                value = mid[x, index]
                for step in range(NX - 1):
                    value = value + x_got[step, index]
                low[index] = value

                @pl.when(index != z)
                def _():
                    remote(
                        low.at[index], z_got.at[z], z_sent, z_came, ctx=ctx_of(x, index, core)
                    ).start()

            return carry

        lax.fori_loop(0, NZ, fold, 0)
    pltpu.make_async_copy(low.at[z], z_got.at[z], z_came).start()
    wait_for(gains_got, gain_sems.at[1])
    gain_total[...] = lax.fori_loop(
        1, count, lambda index, value: value + gains_got[index], gains_got[0]
    )
    wait_for(z_got, z_came)
    value = z_got[0]
    for index in range(1, NZ):
        value = value + z_got[index]
    grad[...] = value
    scan_end(got, came_in, state_sems.at[0], state_sems.at[2], state_sems.at[3])
    wait_for(gains_got.at[pl.ds(0, count - 1)], gain_sems.at[0])
    for step in range(NX):
        wait_for(twin_got.at[step], twin_sems.at[0, step])
    for step in range(NX - 1):
        wait_for(x_got.at[step], x_sent)
    wait_for(z_got.at[pl.ds(0, NZ - 1)], z_sent)


def call(kernel, outs, scratch, ident, *operands):
    vmem = pl.BlockSpec(memory_space=pltpu.VMEM)
    return pl.pallas_call(
        kernel,
        out_shape=outs,
        in_specs=[vmem] * len(operands),
        out_specs=jax.tree.map(lambda _: vmem, outs),
        scratch_shapes=scratch,
        compiler_params=pltpu.CompilerParams(
            collective_id=ident, has_side_effects=True, vmem_limit_bytes=VMEM_LIMIT
        ),
    )(*operands)


def per_device(xin, zin, bmat, cmat, ldec, dskip, gain, w_out, dout):
    f32, bf16 = jnp.float32, jnp.bfloat16
    shape = jax.ShapeDtypeStruct
    dma = pltpu.SemaphoreType.DMA
    blocks, groups = lax.axis_size("ctx"), lax.axis_size("head")
    heads_here, tokens = ldec.shape
    states, width = heads_here * HDIM, bmat.shape[1]
    rows = states // blocks
    inner = xin.shape[1]
    values_x = xin.astype(f32).reshape(tokens, heads_here, HDIM)
    values_b = bmat.astype(f32)
    values_c = cmat.astype(f32)
    positions = jnp.arange(tokens)
    causal = positions[:, None] >= positions[None, :]
    cumlog = jnp.dot(ldec, causal.T.astype(f32), precision=HIGH)
    tail = jnp.exp(cumlog[:, -1:] - cumlog)
    increasing_order = jnp.exp(cumlog)
    local_state = jnp.einsum("ht,thp,tn->hpn", tail, values_x, values_b, precision=HIGH)
    total_decay = jnp.exp(cumlog[:, -1])
    came_in, decays, w_all, dout_all = call(
        first_kernel,
        (
            shape((states, width), f32),
            shape((blocks, 1, width), f32),
            shape((NX, NZ, NC) + w_out.shape, bf16),
            shape((groups,) + dout.shape, bf16),
        ),
        [
            pltpu.VMEM((blocks, rows, width), f32),
            pltpu.VMEM((blocks, rows, width), f32),
            dma((4,)), dma((2,)), dma(()), dma((NZ,)), dma((NX,)), dma((NX,)), dma(()), dma(()),
            dma((2, groups // 2 + 1)),
        ],
        0,
        local_state.reshape(states, width),
        jnp.broadcast_to(total_decay[:, None, None], (heads_here, 1, width)),
        w_out,
        dout,
    )
    incoming_hidden = came_in.reshape(heads_here, HDIM, width)
    columns = jnp.transpose(dout_all, (1, 0, 2)).reshape(tokens, -1)
    normed_grad = jnp.dot(columns, w_all.reshape(-1, inner), preferred_element_type=f32)
    gaps = cumlog[:, :, None] - cumlog[:, None, :]
    decay = jnp.where(causal[None], jnp.exp(jnp.where(causal[None], gaps, 0.0)), 0.0)
    scores = jnp.dot(values_c, values_b.T, precision=HIGH)
    kernel = decay * scores[None]
    inner_out = jnp.einsum("hts,shp->thp", kernel, values_x, precision=HIGH)
    carried = (
        jnp.einsum("hpn,tn->thp", incoming_hidden, values_c, precision=HIGH)
        * increasing_order.T[:, :, None]
    )
    mixed = inner_out + carried + dskip[None, :, None] * values_x
    mixed = mixed.reshape(tokens, -1)
    values_z = zin.astype(f32)
    sigmoid_z = jax.nn.sigmoid(values_z)
    gate_act = values_z * sigmoid_z
    gated = mixed * gate_act
    weighted = gain * normed_grad
    features_all = inner * groups
    sums = jnp.stack([jnp.sum(gated * gated, axis=1), jnp.sum(weighted * gated, axis=1)])
    sums = jnp.pad(sums, ((0, 6), (0, 0)))
    sums = call(
        sum_kernel, shape(sums.shape, f32), [pltpu.VMEM((groups,) + sums.shape, f32), dma(()), dma(())], 1, sums
    )
    inv_rms = lax.rsqrt(sums[0] / features_all + EPSILON)[:, None]
    inner_total = sums[1]
    normed = gated * inv_rms * gain
    gain_part = jnp.sum(normed_grad * gated * inv_rms, axis=0)
    gated_grad = (
        inv_rms * weighted
        - gated * (inv_rms * inv_rms * inv_rms) * (inner_total / features_all)[:, None]
    )
    mixed_grad = gated_grad * gate_act
    grad_z = gated_grad * mixed * sigmoid_z * (1.0 + values_z * (1.0 - sigmoid_z))
    head_grad = mixed_grad.reshape(tokens, heads_here, HDIM)
    skip_part = jnp.sum(head_grad * values_x, axis=(0, 2))
    local_grad = jnp.einsum("ht,thp,tn->hpn", increasing_order, head_grad, values_c, precision=HIGH)
    high = lax.reduce_precision(normed, 8, 7)
    low = (normed - high).astype(bf16)
    grads = lax.dot_general(
        columns, high.astype(bf16), (((0,), (0,)), ((), ())), preferred_element_type=f32
    ) + lax.dot_general(columns, low, (((0,), (0,)), ((), ())), preferred_element_type=f32)
    gain_rows = inner // 128
    small = jnp.concatenate(
        [
            gain_part.reshape(gain_rows, 128),
            jnp.pad(skip_part, (0, 128 - heads_here))[None],
            jnp.zeros((8 - gain_rows - 1, 128), f32),
        ]
    )
    out_rows = w_out.shape[0]
    piece = (out_rows, inner)
    grad_in, grad_w, small = call(
        second_kernel,
        (shape((states, width), f32), shape(piece, f32), shape(small.shape, f32)),
        [
            pltpu.VMEM((blocks, rows, width), f32),
            pltpu.VMEM((blocks, rows, width), f32),
            pltpu.VMEM((NX, NZ) + piece, f32),
            pltpu.VMEM((NX, NZ) + piece, f32),
            pltpu.VMEM((NX - 1, NZ) + piece, f32),
            pltpu.VMEM((NZ,) + piece, f32),
            pltpu.VMEM((NZ,) + piece, f32),
            pltpu.VMEM((blocks,) + small.shape, f32),
            dma((4,)), dma((2,)), dma((2, NX)), dma(()), dma((PARTS, NX)), dma(()), dma(()),
        ],
        2,
        local_grad.reshape(states, width),
        decays,
        grads.reshape((NX, NZ, NC) + piece),
        small,
    )
    grad_in = grad_in.reshape(heads_here, HDIM, width)
    products = jnp.einsum("thp,shp->hts", head_grad, values_x, precision=HIGH) * decay
    grad_x = jnp.einsum("hts,thp->shp", kernel, head_grad, precision=HIGH)
    grad_x = (
        grad_x + jnp.einsum("hpn,sn->shp", grad_in, values_b, precision=HIGH) * tail.T[:, :, None]
    )
    grad_x = grad_x + dskip[None, :, None] * head_grad
    products = jnp.sum(products, axis=0)
    grad_b = jnp.einsum("ts,tn->sn", products, values_c, precision=HIGH)
    grad_b = grad_b + jnp.einsum("hpn,shp,hs->sn", grad_in, values_x, tail, precision=HIGH)
    grad_c = jnp.einsum("ts,sn->tn", products, values_b, precision=HIGH)
    grad_c = grad_c + jnp.einsum(
        "hpn,thp,ht->tn", incoming_hidden, head_grad, increasing_order, precision=HIGH
    )
    shared = jnp.concatenate([grad_b, grad_c])
    share = (shared.shape[0] // groups, width)
    shared = call(
        shared_kernel,
        shape(shared.shape, f32),
        [pltpu.VMEM((groups,) + share, f32), pltpu.VMEM(share, f32), dma((4,))],
        3,
        shared,
    )
    return (
        grad_x.reshape(tokens, -1).astype(bf16),
        grad_z.astype(bf16),
        shared[:tokens],
        shared[tokens:],
        grad_w,
        small[:gain_rows].reshape(-1),
        small[gain_rows, :heads_here],
    )


def solution(mesh):
    return jax.shard_map(
        per_device,
        mesh=mesh,
        in_specs=(
            P("ctx", "head"), P("ctx", "head"), P("ctx", None), P("ctx", None), P("head", "ctx"),
            P("head"), P("head"), P("ctx", "head"), P("ctx", "head"),
        ),
        out_specs=(
            P("ctx", "head"), P("ctx", "head"), P("ctx", None), P("ctx", None), P("ctx", "head"),
            P("head"), P("head"),
        ),
        check_vma=False,
    )
```

time: 622 us -> 166 us (0.27); the launches traced: 613 us -> 164 us
  blocking collectives: 289 us -> 0 us
  other arithmetic: 136 us -> 2.25 us
  Pallas kernels: 0 us -> 125 us
  waiting for transfers between devices: 120 us -> 0 us
  between operations: 15 us -> 0.97 us
  local copies, waits for them, and re-layouts: 27.5 us -> 14.2 us
    psum x3 -> x0, blocking collectives: 157 us -> none  [the longest x1 129 us: per_device(): grad_gain, grad_skip = lax.psum((gain_part, skip_part), 'ctx')]
    select_n x126 -> x0, other arithmetic: 133 us -> none  [turn(): jnp.where(position < mine, new, old)]
    unnamed x1 -> x0, blocking collectives: 132 us -> none
    pallas_call x0 -> x4, Pallas kernels: none -> 125 us  [call(): pl.pallas_call(kernel, out_shape=outs, in_specs=[vmem] * len(operands), o...]
    psum x1 -> x0, waiting for transfers between devices: 78.6 us -> none  [per_device(): grad_b, grad_c = lax.psum((grad_b, grad_c), 'head')]
    unnamed x7 -> x0, waiting for transfers between devices: 25.9 us -> none
    all_gather x4 -> x0, waiting for transfers between devices: 15.4 us -> none  [the longest x1 15.3 us: per_device(): lax.all_gather(w_out, 'ctx', axis=0, tiled=True)]
    rev x2 -> x0, local copies, waits for them, and re-layouts: 12 us -> none  [carried_in(): pieces = jax.tree.map(lambda part: part[::-1], pieces)]
  transfers between devices with their start and end apart: 6 -> 0, of which waited for: 3 -> 0; matrix products, arithmetic and copies ran while one was open for 28% -> 0% of each run, Pallas kernels for 0% -> 0%
where the time goes in v1:
time: 166 us; the launch traced here: 164 us
  Pallas kernels  125 us (75%)
  matrix products  22.2 us (13%)
  local copies, waits for them, and re-layouts  14.2 us (9%)
  other arithmetic  2.25 us (1%)
    pallas_call x4, Pallas kernels, call(): pl.pallas_call(kernel, out_shape=outs, in_specs=[vmem] * len(operands), o...  125 us
    unnamed x39, local copies, waits for them, and re-layouts  6.49 us
    dot_general x1, matrix products, per_device(): inner_out = jnp.einsum('hts,shp->thp', kernel, values_x, precision=HIGH)  3.55 us

profile of v1, /device:TPU:1, one launch (start us, length us, event | category | flops | bytes accessed | tf_op | source)
XLA Modules:
  0.0 164.2 jit_solution(1078968477639954768)
XLA Ops:
  0.6 0.0 copy-start
  0.6 0.9 fusion.53
  1.6 0.2 slice_reduce_fusion
  1.8 0.0 copy-start.16
  1.8 0.1 bitcast_exponential_fusion
  1.9 1.1 copy.31
  3.0 0.0 copy-start.8
  3.0 1.3 fusion.28
  4.3 0.0 copy-done.8
  4.3 0.1 broadcast_in_dim.26.decay
  4.4 0.9 copy-done.2
  5.3 0.8 copy-done.3
  6.1 45.0 %shard_map.144 = (f32[512,128]{1,0:T(8,128)S(1)}, f32[64,1,128]{2,1,0:T(1,128)S(1)}, bf16[4,8,2,32,512]{4,3,2,1,0:T(8,128)(2,1)S(1)}, bf16[8,256,256]{2,1,0:T(8,128)(2,1)S(1)}) custom-call(f32[512,128]{1,0:T(8,128)S(1)} %bitcast.96, f32[8,1,128]{2,1,0:T(1,128)S(1)} %broadcast_in_dim.26.decay, bf16[32,512]{1,0:T(8,128)(2,1)S(1)} %copy-done.3, ...), custom_call_target="tpu_custom_call" | custom-call | tf_op jit(solution)/shard_map/pallas_call | solution.py:309
  51.2 0.0 copy-done
  51.2 0.0 copy-start.13
  51.2 1.0 fusion.65
  52.2 0.0 copy-done.16
  52.2 0.0 copy-start.11
  52.3 3.6 %fusion.5 = f32[256,8,64]{0,2,1:T(8,128)} fusion(bf16[256,8,64]{0,2,1:T(8,128)(2,1)} %bitcast.112, f32[256,256]{1,0:T(8,128)S(1)} %fusion.65, f32[8,256]{1,0:T(8,128)S(1)} %bitcast.120, pred[256,256]{1,0:T(8,128)(4,1)S(1)} %iota_compare_fusion), kind=kOutput, calls=%fused_computation.6 | convolution fusion | flops 404750336 | bytes 1122304 | tf_op jit(solution)/shard_map/hts,shp->thp/dot_general | solution.py:367
  55.8 0.0 copy-done.13
  55.8 0.0 copy-done.11
  55.8 0.7 subtract_exponential_fusion
  56.5 1.9 %copy.32 = f32[256,512]{0,1:T(8,128)} copy(bf16[256,512]{1,0:T(8,128)(2,1)} %param.9) | data formatting | bytes 786432 | tf_op jit(solution)/shard_map/convert_element_type | solution.py:330
  58.4 2.4 %fusion.13 = f32[256,8,64]{0,2,1:T(8,128)} fusion(f32[256,8,64]{0,2,1:T(8,128)} %fusion.5, f32[8,64,128]{2,1,0:T(8,128)S(1)} %bitcast.98, f32[256,8,64]{0,2,1:T(8,128)} %bitcast.116, f32[8]{0:T(128)} %param.14, f32[256,8]{0,1:T(8,128)S(1)} %get-tuple-element.54, bf16[256,128]{1,0:T(8,128)(2,1)S(1)} %copy-done), kind=kOutput, calls=%fused_computation.12 | convolution fusion | flops 201850880 | bytes 1908768 | tf_op jit(solution)/shard_map/hpn,tn->thp/dot_general | solution.py:369
  60.8 2.1 %copy.33 = f32[256,512]{1,0:T(8,128)} copy(f32[256,512]{0,1:T(8,128)} %bitcast.115) | data formatting | bytes 1048576 | tf_op jit(solution)/shard_map/reshape | solution.py:373
  62.9 1.3 copy.34
  64.2 0.0 copy-done.15
  64.2 2.4 %multiply_reduce_fusion.4 = (f32[256]{0:T(256)S(1)}, f32[256]{0:T(256)S(1)}, f32[256,512]{1,0:T(8,128)S(1)}) fusion(f32[256,512]{1,0:T(8,128)} %copy.33, bf16[256,512]{1,0:T(8,128)(2,1)} %param.10, f32[512]{0:T(512)S(1)} %copy-done.15, bf16[256,2048]{0,1:T(8,128)(2,1)} %bitcast.103, bf16[2048,512]{1,0:T(8,128)(2,1)S(1)} %bitcast.102), kind=kOutput, calls=%fused_computation.55 | convolution fusion | flops 538312192 | bytes 4460544 | tf_op jit(solution)/shard_map/dot_general | solution.py:362
  66.6 7.5 %shard_map.145 = f32[8,256]{1,0:T(8,128)S(1)} custom-call(f32[8,256]{1,0:T(8,128)S(1)} %select_maximum_fusion.part), custom_call_target="tpu_custom_call" | custom-call | tf_op jit(solution)/shard_map/pallas_call | solution.py:309
  74.1 0.0 copy-done.4
  74.1 0.0 copy-done.5
  74.1 0.0 copy-done.6
  74.1 0.9 fusion.42
  75.0 0.0 copy-start.7
  75.0 2.8 %convolution_add_fusion = f32[2048,512]{1,0:T(8,128)} fusion(f32[2048,512]{1,0:T(8,128)S(1)} %fusion.42, bf16[256,2048]{0,1:T(8,128)(2,1)S(1)} %bitcast.105, f32[256]{0:T(256)S(1)} %bitcast.124, f32[512]{0:T(512)S(1)} %copy-done.15, f32[256,512]{1,0:T(8,128)S(1)} %copy-done.5, bf16[256,512]{1,0:T(8,128)(2,1)S(1)} %copy-done.6), kind=kOutput, calls=%fused_computation | convolution fusion | flops 539361280 | bytes 10226688 | tf_op jit(solution)/shard_map/dot_general | solution.py:402
  77.9 0.0 copy-done.7
  77.9 1.2 multiply_reduce_fusion.1
  79.1 0.1 reduce_sum.56
  79.1 0.1 reduce_sum.57
  79.3 0.1 pad.14.clone
  79.3 0.1 maximum_maximum_fusion.gains
  79.4 0.2 copy.35
  79.6 0.4 fusion.39
  80.0 0.0 copy-start.1
  80.0 2.2 %copy-done.1 = f32[2048,512]{1,0:T(8,128)S(1)} copy-done((f32[2048,512]{1,0:T(8,128)S(1)}, f32[2048,512]{1,0:T(8,128)}, u32[]{:S(2)}) %copy-start.1) | copy-done | bytes 4194328
  82.2 54.0 %shard_map.146 = (f32[512,128]{1,0:T(8,128)S(1)}, f32[32,512]{1,0:T(8,128)S(1)}, f32[8,128]{1,0:T(8,128)S(1)}) custom-call(f32[512,128]{1,0:T(8,128)S(1)} %bitcast.95, f32[64,1,128]{2,1,0:T(1,128)S(1)} %get-tuple-element.17.decays, f32[4,8,2,32,512]{4,3,2,1,0:T(8,128)S(1)} %bitcast.94, f32[8,128]{1,0:T(8,128)S(1)} %maximum_maximum_fusion.gains), custom_call_target="tpu_custom_call" | custom-call | tf_op jit(solution)/shard_map/pallas_call | solution.py:309
  136.2 0.0 copy-done.9
  136.2 1.0 convolution_bitcast_fusion.3
  137.2 0.0 copy-start.10
  137.2 1.5 multiply_reduce_fusion
  138.8 0.4 convolution_add_fusion.2
  139.2 1.0 convolution_bitcast_fusion.2
  140.2 0.0 copy-done.10
  140.2 0.3 convolution_add_fusion.1
  140.5 18.1 %shard_map.147 = f32[512,128]{1,0:T(8,128)S(1)} custom-call(f32[512,128]{1,0:T(8,128)S(1)} %pad_maximum_fusion.part), custom_call_target="tpu_custom_call" | custom-call | tf_op jit(solution)/shard_map/pallas_call | solution.py:309
  158.6 0.0 copy-start.17
  158.6 0.7 fusion.64
  159.3 1.9 %fusion.8 = f32[256,8,64]{0,2,1:T(8,128)S(1)} fusion(f32[256,8,64]{0,2,1:T(8,128)S(1)} %bitcast.109, f32[256,256]{1,0:T(8,128)S(1)} %copy-done.12, f32[8,256]{1,0:T(8,128)S(1)} %bitcast.122, pred[256,256]{1,0:T(8,128)(4,1)S(1)} %copy-done.14), kind=kOutput, calls=%fused_computation.7 | convolution fusion | flops 404750336 | bytes 1384448 | tf_op jit(solution)/shard_map/hts,thp->shp/dot_general | solution.py:435
  161.2 0.0 copy-done.17
  161.2 0.4 fusion.17
  161.6 0.8 copy.37
  162.5 0.6 slice_bitcast_fusion
  163.1 0.5 slice_bitcast_fusion.1
  163.6 0.6 copy.39
  (19 shorter events, 0.1 us)
Async XLA Ops:
  0.6 50.5 %copy-start = (bf16[256,128]{1,0:T(8,128)(2,1)S(1)}, bf16[256,128]{1,0:T(8,128)(2,1)}, u32[]{:S(2)}) copy-start(bf16[256,128]{1,0:T(8,128)(2,1)} %param.12) | copy-start | bytes 196612
  1.8 50.4 %copy-start.16 = (f32[8]{0:T(128)}, f32[8]{0:T(128)S(1)}, u32[]{:S(2)}) copy-start(f32[8]{0:T(128)S(1)} %slice_reduce_fusion) | copy-start | bytes 100
  3.0 1.3 copy-start.8
  4.4 0.9 copy-start.2
  5.3 0.8 copy-start.3
  51.2 4.6 %copy-start.13 = (pred[256,256]{1,0:T(8,128)(4,1)}, pred[256,256]{1,0:T(8,128)(4,1)S(1)}, u32[]{:S(2)}) copy-start(pred[256,256]{1,0:T(8,128)(4,1)S(1)} %iota_compare_fusion) | copy-start | bytes 196612
  52.2 3.6 %copy-start.11 = (f32[256,256]{1,0:T(8,128)}, f32[256,256]{1,0:T(8,128)S(1)}, u32[]{:S(2)}) copy-start(f32[256,256]{1,0:T(8,128)S(1)} %fusion.65) | copy-start | bytes 786436
  60.8 3.4 %copy-start.15 = (f32[512]{0:T(512)S(1)}, f32[512]{0:T(512)}, u32[]{:S(2)}) copy-start(f32[512]{0:T(512)} %param.15) | copy-start | bytes 6148
  64.2 10.0 %copy-start.4 = (bf16[256,8,256]{0,2,1:T(8,128)(2,1)S(1)}, bf16[256,8,256]{0,2,1:T(8,128)(2,1)}, u32[]{:S(2)}) copy-start(bf16[256,8,256]{0,2,1:T(8,128)(2,1)} %copy.34) | copy-start | bytes 3145732
  64.2 10.0 %copy-start.5 = (f32[256,512]{1,0:T(8,128)S(1)}, f32[256,512]{1,0:T(8,128)}, u32[]{:S(2)}) copy-start(f32[256,512]{1,0:T(8,128)} %copy.33) | copy-start | bytes 1572868
  64.2 10.0 %copy-start.6 = (bf16[256,512]{1,0:T(8,128)(2,1)S(1)}, bf16[256,512]{1,0:T(8,128)(2,1)}, u32[]{:S(2)}) copy-start(bf16[256,512]{1,0:T(8,128)(2,1)} %param.10) | copy-start | bytes 786436
  75.0 2.8 %copy-start.7 = (bf16[256,512]{1,0:T(8,128)(2,1)S(1)}, bf16[256,512]{1,0:T(8,128)(2,1)}, u32[]{:S(2)}) copy-start(bf16[256,512]{1,0:T(8,128)(2,1)} %param.9) | copy-start | bytes 786436
  80.0 2.2 %copy-start.1 = (f32[2048,512]{1,0:T(8,128)S(1)}, f32[2048,512]{1,0:T(8,128)}, u32[]{:S(2)}) copy-start(f32[2048,512]{1,0:T(8,128)} %convolution_add_fusion) | copy-start | bytes 12582916
  82.2 54.0 %copy-start.9 = (bf16[256,512]{0,1:T(8,128)(2,1)S(1)}, bf16[256,512]{0,1:T(8,128)(2,1)}, u32[]{:S(2)}) copy-start(bf16[256,512]{0,1:T(8,128)(2,1)} %copy-done.8) | copy-start | bytes 786436
  82.2 55.0 %copy-start.14 = (pred[256,256]{1,0:T(8,128)(4,1)S(1)}, pred[256,256]{1,0:T(8,128)(4,1)}, u32[]{:S(2)}) copy-start(pred[256,256]{1,0:T(8,128)(4,1)} %copy-done.13) | copy-start | bytes 196612
  137.2 3.0 %copy-start.10 = (bf16[256,128]{1,0:T(8,128)(2,1)S(1)}, bf16[256,128]{1,0:T(8,128)(2,1)}, u32[]{:S(2)}) copy-start(bf16[256,128]{1,0:T(8,128)(2,1)} %param.11) | copy-start | bytes 196612
  138.8 20.5 %copy-start.12 = (f32[256,256]{1,0:T(8,128)S(1)}, f32[256,256]{1,0:T(8,128)}, u32[]{:S(2)}) copy-start(f32[256,256]{1,0:T(8,128)} %copy-done.11) | copy-start | bytes 786436
  158.6 2.6 %copy-start.17 = (f32[8]{0:T(128)S(1)}, f32[8]{0:T(128)}, u32[]{:S(2)}) copy-start(f32[8]{0:T(128)} %param.14) | copy-start | bytes 100

commit v2 on v0

v2 whole, which is shorter than its diff:
```python
import types
import jax
import jax.numpy as jnp
from jax import lax
from jax.experimental import pallas as pl
from jax.experimental.pallas import tpu as pltpu
from jax.sharding import PartitionSpec as P

HDIM = 64
HIGH = lax.Precision.HIGHEST
EPSILON = 1e-05
MESH = pl.DeviceIdType.MESH
NX, NZ, NC = 4, 8, 2
PARTS = 2
LANES = 128
CHUNK = 16
VMEM_LIMIT = 56 * 2**20
f32, bf16 = jnp.float32, jnp.bfloat16


def remote(src, dst, sent, came, **where):
    return pltpu.make_async_remote_copy(
        src_ref=src, dst_ref=dst, send_sem=sent, recv_sem=came, device_id=where, device_id_type=MESH
    )


def local(src, dst, sem):
    return pltpu.make_async_copy(src, dst, sem)


def wait_for(ref, sem):
    local(ref, ref, sem).wait()


def others(axis, act):
    count, mine = lax.axis_size(axis), lax.axis_index(axis)

    def turn(step, carry):
        act(lax.rem(mine + step, count))
        return carry

    lax.fori_loop(1, count, turn, 0)


def ctx_of(x, z, core):
    return (x * NZ + z) * NC + core


def split(value):
    high = value.astype(bf16)
    return high, (value - high.astype(f32)).astype(bf16)


def dot(a, b):
    return jnp.dot(a, b, preferred_element_type=f32)


def dot_nt(a, b, precision=None):
    return lax.dot_general(
        a, b, (((1,), (1,)), ((), ())), preferred_element_type=f32, precision=precision
    )


def rows_at(ref, index, rows):
    return ref.at[pl.ds(pl.multiple_of(index * rows, rows), rows)]


def loop(count, body):
    def turn(index, carry):
        body(index)
        return carry

    lax.fori_loop(0, count, turn, 0)


def scan_send(state, got, sent, came):
    mine, rows = lax.axis_index("ctx"), got.shape[1]
    others(
        "ctx",
        lambda peer: remote(rows_at(state, peer, rows), got.at[mine], sent, came, ctx=peer).start(),
    )
    local(rows_at(state, mine, rows), got.at[mine], came).start()


def scan_turn(got, decays, before, out, sent, came, came_back, backward):
    mine = lax.axis_index("ctx")
    count, rows = got.shape[0], got.shape[1]
    head = mine // (HDIM // rows)
    wait_for(got, came)

    def turn(step, total):
        index = count - 1 - step if backward else step
        before[index] = total
        factor = decays[
            index // (NZ * NC), lax.rem(index // NC, NZ), lax.rem(index, NC), head
        ]
        return factor * total + got[index]

    lax.fori_loop(0, count, turn, jnp.zeros(got.shape[1:], f32), unroll=4)
    home = rows_at(out, mine, rows)
    others("ctx", lambda peer: remote(before.at[peer], home, sent, came_back, ctx=peer).start())
    local(before.at[mine], home, came_back).start()


def shared_send(part, got, sems):
    mine, rows = lax.axis_index("head"), got.shape[1]
    others(
        "head",
        lambda peer: remote(rows_at(part, peer, rows), got.at[mine], sems.at[0], sems.at[1], head=peer).start(),
    )
    local(rows_at(part, mine, rows), got.at[mine], sems.at[1]).start()


def shared_turn(got, summed, total, sems):
    mine, rows = lax.axis_index("head"), got.shape[1]
    wait_for(got, sems.at[1])
    value = got[0]
    for index in range(1, got.shape[0]):
        value = value + got[index]
    summed[...] = value
    home = rows_at(total, mine, rows)
    others("head", lambda peer: remote(summed, home, sems.at[2], sems.at[3], head=peer).start())
    local(summed, home, sems.at[3]).start()


def shared_end(got, total, sems):
    peers = got.at[pl.ds(0, got.shape[0] - 1)]
    wait_for(total, sems.at[3])
    wait_for(peers, sems.at[0])
    wait_for(peers, sems.at[2])


def whole_kernel(names, *refs):
    r = types.SimpleNamespace(**dict(zip(names, refs)))
    mine, row = lax.axis_index("ctx"), lax.axis_index("head")
    count, groups = lax.axis_size("ctx"), lax.axis_size("head")
    x, z, core = mine // (NZ * NC), lax.rem(mine // NC, NZ), lax.rem(mine, NC)
    twin = ctx_of(x, z, 1 - core)
    heads, tokens = r.ldec.shape
    pairs = heads // 2
    inner = heads * HDIM
    half = tokens // 2
    features = inner * groups
    chunks = tokens // CHUNK
    first_head = lax.broadcasted_iota(jnp.int32, (tokens, LANES), 1) < HDIM

    def pair_lanes(pair):
        return pl.ds(pl.multiple_of(pair * LANES, LANES), LANES)

    def chunk_rows(chunk):
        return pl.ds(pl.multiple_of(chunk * CHUNK, CHUNK), CHUNK)

    barrier = pltpu.get_barrier_semaphore()
    for axis in ("ctx", "head"):
        others(
            axis,
            lambda peer: pl.semaphore_signal(
                barrier, inc=1, device_id={axis: peer}, device_id_type=MESH
            ),
        )

    token_of = lax.broadcasted_iota(jnp.int32, (tokens, tokens), 0)
    other_of = lax.broadcasted_iota(jnp.int32, (tokens, tokens), 1)
    logs = dot_nt(r.ldec[...], (token_of >= other_of).astype(f32), HIGH)
    columns = jnp.transpose(logs)
    for head in range(heads):
        r.cum[head] = logs[head : head + 1]
        r.col[head] = jnp.broadcast_to(columns[:, head : head + 1], (tokens, LANES))
    for head in range(heads):
        r.decays[x, z, core, head] = jnp.exp(r.col[head, tokens - 1 : tokens, :])

    def local_states(pair):
        lanes = pair_lanes(pair)
        log = jnp.where(first_head, r.col[2 * pair], r.col[2 * pair + 1])
        tail = jnp.exp(log[tokens - 1 :] - log)
        r.tail[:, lanes] = tail
        r.inc[:, lanes] = jnp.exp(log)
        high, low = split(jnp.transpose(r.x[:, lanes].astype(f32) * tail))
        r.state[pl.ds(pl.multiple_of(pair * LANES, LANES), LANES)] = dot(high, r.b[...]) + dot(
            low, r.b[...]
        )

    loop(pairs, local_states)
    pl.semaphore_wait(barrier, count + groups - 2)

    scan_send(r.state, r.got, r.state_sems.at[0], r.state_sems.at[1])
    for step in range(1, NZ):
        peer = ctx_of(x, lax.rem(z + step, NZ), core)
        remote(r.decays.at[x, z, core], r.decays.at[x, z, core], r.decay_sent, r.decay_z.at[step], ctx=peer).start()
    w_home = local(r.w, r.w_all.at[x, z, core], r.w_own)
    w_home.start()
    for step in range(1, NZ):
        peer = ctx_of(x, lax.rem(z + step, NZ), core)
        remote(r.w, r.w_all.at[x, z, core], r.w_sent, r.w_z.at[step], ctx=peer).start()
    for turn in range(NX - 1):
        peer = ctx_of(lax.rem(x + turn + 1, NX), z, core)
        remote(r.w, r.w_all.at[x, z, core], r.w_sent, r.w_x.at[turn], ctx=peer).start()
    right, left = lax.rem(row + 1, groups), lax.rem(row + groups - 1, groups)
    far, near = groups // 2, groups - 1 - groups // 2

    def ring(step):
        for side, most, target, back in ((0, far, right, -step), (1, near, left, step)):
            if step < most:
                piece = lax.rem(row + groups + back, groups)
                if step:
                    wait_for(r.dout_all.at[piece], r.d_came.at[side, step])
                source = r.dout_all.at[piece] if step else r.dout
                remote(
                    source, r.dout_all.at[piece], r.d_sent, r.d_came.at[side, step + 1], head=target
                ).start()

    ring(0)

    scores = dot_nt(r.c[...], r.b[...])
    r.scores[...] = scores
    causal = (
        lax.broadcasted_iota(jnp.int32, (half, half), 0)
        >= lax.broadcasted_iota(jnp.int32, (half, half), 1)
    )

    def inside(pair):
        lanes = pair_lanes(pair)
        parts = []
        for head in (2 * pair, 2 * pair + 1):
            outs = []
            for top in (0, 1):
                high, low = [], []
                at = pl.ds(top * half, half)
                for side in range(top + 1):
                    to = pl.ds(side * half, half)
                    gap = r.col[head, at, :] - r.cum[head, :, to]
                    if side == top:
                        decay = jnp.where(causal, jnp.exp(jnp.where(causal, gap, 0.0)), 0.0)
                    else:
                        decay = jnp.exp(gap)
                    r.decay[head, at, to] = decay
                    h, l = split(decay * r.scores[at, to])
                    r.kern_high[head, at, to] = h
                    r.kern_low[head, at, to] = l
                    high.append(h)
                    low.append(l)
                values = r.x[pl.ds(0, (top + 1) * half), lanes]
                outs.append(
                    dot(jnp.concatenate(high, axis=1), values) + dot(jnp.concatenate(low, axis=1), values)
                )
            parts.append(jnp.concatenate(outs, axis=0))
        r.mixed[:, lanes] = jnp.where(first_head, parts[0], parts[1]) + r.skip[:, lanes] * r.x[
            :, lanes
        ].astype(f32)

    def gate(chunk):
        at = chunk_rows(chunk)
        value = r.z[at, :].astype(f32)
        sigmoid = 1.0 / (1.0 + jnp.exp(-value))
        r.act[at, :] = value * sigmoid
        r.slope[at, :] = sigmoid * (1.0 + value * (1.0 - sigmoid))

    def relay(step):
        source = lax.rem(z + NZ - step, NZ)
        wait_for(r.w_all.at[x, source, core], r.w_z.at[step])
        for turn in range(NX - 1):
            peer = ctx_of(lax.rem(x + turn + 1, NX), z, core)
            piece = r.w_all.at[x, source, core]
            remote(piece, piece, r.w_sent, r.w_x.at[turn], ctx=peer).start()

    loop(pairs // 2, inside)
    spot = x * NC + core
    for step in range(1, NZ):
        wait_for(r.decays.at[x, lax.rem(z + NZ - step, NZ), core], r.decay_z.at[step])
    for step in range(1, NX * NC):
        other = lax.rem(spot + step, NX * NC)
        line = r.decays.at[x, :, core]
        remote(
            line, line, r.decay_sent, r.decay_x.at[step], ctx=ctx_of(other // NC, z, lax.rem(other, NC))
        ).start()
    for step in range(1, NZ):
        relay(step)
        if step % 2 == 0:
            ring(step // 2)
    w_home.wait()
    mine_line = r.w_all.at[x, :, core]
    remote(mine_line, mine_line, r.w_sent, r.w_core.at[0], ctx=twin).start()
    for step in range(1, NX * NC):
        other = lax.rem(spot + NX * NC - step, NX * NC)
        wait_for(r.decays.at[other // NC, :, lax.rem(other, NC)], r.decay_x.at[step])
    scan_turn(
        r.got, r.decays, r.before, r.came_in, r.state_sems.at[2], r.state_sems.at[1], r.state_sems.at[3],
        False,
    )
    for step in range(1, far):
        if step > (NZ - 1) // 2:
            ring(step)
    for turn in range(NX - 1):
        line = r.w_all.at[lax.rem(x + NX - turn - 1, NX), :, core]
        wait_for(line, r.w_x.at[turn])
        remote(line, line, r.w_sent, r.w_core.at[turn + 1], ctx=twin).start()
    lax.fori_loop(pairs // 2, pairs, lambda pair, carry: (inside(pair), carry)[1], 0)
    loop(chunks, gate)
    r.dout_all[row] = r.dout[...]
    wait_for(r.dout_all.at[lax.rem(row + groups - far, groups)], r.d_came.at[0, far])
    if near:
        wait_for(r.dout_all.at[lax.rem(row + near, groups)], r.d_came.at[1, near])

    def turned(piece):
        r.dout_turned[piece] = jnp.transpose(r.dout_all[piece])

    loop(groups, turned)
    for turn in range(NX):
        wait_for(r.w_all.at[lax.rem(x + NX - turn, NX), :, 1 - core], r.w_core.at[turn])
    piece_rows, piece_width = r.w.shape[0], r.dout.shape[1]
    deep = piece_width // (piece_rows * NC)
    line_pieces = NZ // deep

    def project(piece):
        z_from = pl.ds(lax.rem(piece, line_pieces) * deep, deep)
        block = r.w_all[piece // line_pieces, z_from].reshape(piece_width, inner)
        value = dot(r.dout_all[piece], block)

        @pl.when(piece == 0)
        def _():
            r.normed_grad[...] = value

        @pl.when(piece > 0)
        def _():
            r.normed_grad[...] += value

    loop(groups, project)

    wait_for(r.came_in, r.state_sems.at[3])
    in_high, in_low = split(r.came_in[...])
    r.carried[...] = dot_nt(r.c[...], in_high) + dot_nt(r.c[...], in_low)

    def gated_rows(chunk):
        at = chunk_rows(chunk)
        mixed = r.mixed[at, :] + r.carried[at, :] * r.inc[at, :]
        gated = mixed * r.act[at, :]
        r.mixed[at, :] = mixed
        r.gated[at, :] = gated
        square = gated * gated
        product = r.gain[...] * r.normed_grad[at, :] * gated
        fold = lambda value: sum(
            value[:, lane : lane + LANES] for lane in range(LANES, inner, LANES)
        ) + value[:, :LANES]
        r.square[at, :] = fold(square)
        r.product[at, :] = fold(product)

    loop(chunks, gated_rows)
    ones = jnp.ones((8, LANES), f32)
    top_row = lax.broadcasted_iota(jnp.int32, (8, tokens), 0) == 0
    r.sums[...] = jnp.where(
        top_row, dot_nt(ones, r.square[...], HIGH), dot_nt(ones, r.product[...], HIGH)
    )
    others(
        "head", lambda peer: remote(r.sums, r.sums_got.at[row], r.sum_sems.at[0], r.sum_sems.at[1], head=peer).start()
    )
    local(r.sums, r.sums_got.at[row], r.sum_sems.at[1]).start()
    wait_for(r.sums_got, r.sum_sems.at[1])
    total = r.sums_got[0]
    for index in range(1, groups):
        total = total + r.sums_got[index]
    inv = lax.rsqrt(total[0:1] / features + EPSILON)
    pull = inv * inv * inv * (total[1:2] / features)
    both = jnp.transpose(jnp.where(top_row, inv, pull))
    r.inv[...] = jnp.broadcast_to(both[:, 0:1], (tokens, LANES))
    r.pull[...] = jnp.broadcast_to(both[:, 1:2], (tokens, LANES))

    def gradient_rows(chunk, sums):
        at = chunk_rows(chunk)
        wide = lambda value: jnp.concatenate([value] * (inner // LANES), axis=1)
        inv, pull = wide(r.inv[at, :]), wide(r.pull[at, :])
        gated, normed_grad = r.gated[at, :], r.normed_grad[at, :]
        scaled = gated * inv
        r.normed_high[at, :], r.normed_low[at, :] = split(scaled * r.gain[...])
        gated_grad = inv * (r.gain[...] * normed_grad) - gated * pull
        grad = gated_grad * r.act[at, :]
        r.grad_z[at, :] = (gated_grad * r.mixed[at, :] * r.slope[at, :]).astype(bf16)
        r.grad[at, :] = grad
        r.grad_inc[at, :] = grad * r.inc[at, :]
        gain = normed_grad * scaled
        skip = grad * r.x[at, :].astype(f32)
        fold = lambda value: sum(value[at : at + 8] for at in range(8, CHUNK, 8)) + value[:8]
        return sums[0] + fold(gain), sums[1] + fold(skip)

    zero = jnp.zeros((8, inner), f32)
    gain_sum, skip_sum = lax.fori_loop(0, chunks, gradient_rows, (zero, zero))
    gain_sum = jnp.sum(gain_sum, axis=0, keepdims=True)
    skip_sum = jnp.sum(skip_sum, axis=0, keepdims=True)
    for index in range(pairs):
        lanes = slice(index * LANES, (index + 1) * LANES)
        r.small[index : index + 1, :] = gain_sum[:, lanes]
        r.small[pairs + index : pairs + index + 1, :] = skip_sum[:, lanes]

    all_but_one = r.got.at[pl.ds(0, count - 1)]
    wait_for(all_but_one, r.state_sems.at[0])
    wait_for(all_but_one, r.state_sems.at[2])

    def local_gradients(pair):
        lanes = pair_lanes(pair)
        high, low = split(jnp.transpose(r.grad_inc[:, lanes]))
        r.state_grad[pl.ds(pl.multiple_of(pair * LANES, LANES), LANES)] = dot(high, r.c[...]) + dot(
            low, r.c[...]
        )

    loop(pairs, local_gradients)
    scan_send(r.state_grad, r.got_grad, r.back_sems.at[0], r.back_sems.at[1])

    order = [lax.rem(x + step, NX) for step in range(1, NX + 1)]
    depth = NZ // PARTS
    for step in range(NX):
        left_side = jnp.concatenate(
            [r.dout_turned[order[step] * line_pieces + index] for index in range(line_pieces)], axis=0
        )
        value = dot(left_side, r.normed_high[...]) + dot(left_side, r.normed_low[...])
        r.grads[order[step]] = value.reshape(NZ, NC, piece_rows, inner)
        remote(
            r.grads.at[order[step], :, 1 - core], r.twin_got.at[order[step]], r.twin_sems.at[0, step],
            r.twin_sems.at[1, step], ctx=twin,
        ).start()
    others(
        "ctx", lambda peer: remote(r.small, r.small_got.at[mine], r.small_sems.at[0], r.small_sems.at[1], ctx=peer).start()
    )
    local(r.small, r.small_got.at[mine], r.small_sems.at[1]).start()
    for step in range(NX):
        wait_for(r.twin_got.at[order[step]], r.twin_sems.at[1, step])

        def add(index):
            r.mid[order[step], index] = (
                r.grads[order[step], index, core] + r.twin_got[order[step], index]
            )

        loop(NZ, add)
        if step < NX - 1:
            for part in range(PARTS):
                block = pl.ds(part * depth, depth)
                remote(
                    r.mid.at[order[step], block], r.x_got.at[step, block], r.x_sent,
                    r.x_came.at[part, step], ctx=ctx_of(order[step], z, core),
                ).start()

    def products(pair):
        lanes = pair_lanes(pair)
        grad = r.grad[:, lanes]
        high, low = split(grad)
        both = jnp.concatenate([high, low], axis=1)
        values = r.x[:, lanes].astype(f32)
        turned_high, turned_low = split(jnp.transpose(grad))
        outs = []
        for side in (0, 1):
            head = 2 * pair + side
            masked = jnp.where(first_head == (side == 0), values, 0.0).astype(bf16)
            masked = jnp.concatenate([masked, masked], axis=1)
            for top in (0, 1):
                at, to = pl.ds(top * half, half), pl.ds(0, (top + 1) * half)
                value = dot_nt(both[top * half : (top + 1) * half], masked[: (top + 1) * half])
                r.products[at, to] += value * r.decay[head, at, to]
            mine_high = turned_high[side * HDIM : (side + 1) * HDIM]
            mine_low = turned_low[side * HDIM : (side + 1) * HDIM]
            lines = []
            for to in (0, 1):
                at, lane = pl.ds(to * half, tokens - to * half), pl.ds(to * half, half)
                kern = r.kern_high[head, at, lane]
                lines.append(
                    dot(mine_high[:, to * half :], kern)
                    + dot(mine_low[:, to * half :], kern)
                    + dot(mine_high[:, to * half :], r.kern_low[head, at, lane])
                )
            outs.append(jnp.concatenate(lines, axis=1))
        r.grad_values[:, lanes] = jnp.transpose(jnp.concatenate(outs, axis=0)) + r.skip[:, lanes] * grad

    r.products[...] = jnp.zeros_like(r.products)
    loop(pairs, products)
    high, low = split(r.products[...])
    in_high, in_low = split(r.came_in[...])
    out_high, out_low = split(r.grad_inc[...])
    r.part_c[...] = (
        dot(high, r.b[...]) + dot(low, r.b[...])
        + dot(out_high, in_high) + dot(out_low, in_high) + dot(out_high, in_low)
    )
    shared_send(r.part_c, r.got_c, r.c_sems)
    high, low = split(jnp.transpose(r.products[...]))
    r.part_b[...] = dot(high, r.c[...]) + dot(low, r.c[...])

    scan_turn(
        r.got_grad, r.decays, r.before_grad, r.grad_in, r.back_sems.at[2], r.back_sems.at[1],
        r.back_sems.at[3], True,
    )
    shared_turn(r.got_c, r.sum_c, r.grad_c, r.c_sems)

    def fold_part(part):
        block = pl.ds(part * depth, depth)
        for step in range(NX - 1):
            wait_for(r.x_got.at[step, block], r.x_came.at[part, step])

        def fold(turn):
            index = lax.rem(z + turn + 1, NZ)

            @pl.when((index >= part * depth) & (index < (part + 1) * depth))
            def _():
                value = r.mid[x, index]
                for step in range(NX - 1):
                    value = value + r.x_got[step, index]
                r.low[index] = value

                @pl.when(index != z)
                def _():
                    remote(
                        r.low.at[index], r.z_got.at[z], r.z_sent, r.z_came, ctx=ctx_of(x, index, core)
                    ).start()

        loop(NZ, fold)

    fold_part(0)
    wait_for(r.grad_in, r.back_sems.at[3])
    in_high, in_low = split(r.grad_in[...])
    r.carried[...] = dot_nt(r.b[...], in_high) + dot_nt(r.b[...], in_low)

    def weigh(chunk):
        at = chunk_rows(chunk)
        tail = r.tail[at, :]
        r.grad_x[at, :] = (r.grad_values[at, :] + r.carried[at, :] * tail).astype(bf16)
        r.grad_inc[at, :] = r.x[at, :].astype(f32) * tail

    loop(chunks, weigh)
    out_high, out_low = split(r.grad_inc[...])
    r.part_b[...] += dot(out_high, in_high) + dot(out_low, in_high) + dot(out_high, in_low)
    shared_send(r.part_b, r.got_b, r.b_sems)
    for part in range(1, PARTS):
        fold_part(part)
    local(r.low.at[z], r.z_got.at[z], r.z_came).start()
    shared_turn(r.got_b, r.sum_b, r.grad_b, r.b_sems)
    wait_for(r.small_got, r.small_sems.at[1])
    r.small_total[...] = lax.fori_loop(
        1, count, lambda index, value: value + r.small_got[index], r.small_got[0]
    )
    wait_for(r.z_got, r.z_came)
    value = r.z_got[0]
    for index in range(1, NZ):
        value = value + r.z_got[index]
    r.grad_w[...] = value

    shared_end(r.got_c, r.grad_c, r.c_sems)
    shared_end(r.got_b, r.grad_b, r.b_sems)
    wait_for(all_but_one, r.back_sems.at[0])
    wait_for(all_but_one, r.back_sems.at[2])
    wait_for(r.small_got.at[pl.ds(0, count - 1)], r.small_sems.at[0])
    for step in range(NX):
        wait_for(r.twin_got.at[step], r.twin_sems.at[0, step])
    for step in range(NX - 1):
        wait_for(r.x_got.at[step], r.x_sent)
    wait_for(r.z_got.at[pl.ds(0, NZ - 1)], r.z_sent)
    wait_for(r.dout_all.at[pl.ds(0, groups - 1)], r.d_sent)
    wait_for(r.sums_got.at[pl.ds(0, groups - 1)], r.sum_sems.at[0])
    wait_for(r.decays.at[0, pl.ds(0, NZ - 1), 0], r.decay_sent)
    for step in range(1, NX * NC):
        wait_for(r.decays.at[0, :, 0], r.decay_sent)
    for turn in range(2 * NX - 1):
        wait_for(r.w_all.at[turn % NX, :, 0], r.w_sent)
    wait_for(r.w_all.at[0, pl.ds(0, NZ - 1), 0], r.w_sent)


def per_device(xin, zin, bmat, cmat, ldec, dskip, gain, w_out, dout):
    shape = jax.ShapeDtypeStruct
    dma = pltpu.SemaphoreType.DMA
    blocks, groups = lax.axis_size("ctx"), lax.axis_size("head")
    heads, tokens = ldec.shape
    inner, width = heads * HDIM, bmat.shape[1]
    rows, share = inner // blocks, tokens // groups
    piece = w_out.shape
    wide = pltpu.VMEM((tokens, inner), f32)
    wide_half = pltpu.VMEM((tokens, inner), bf16)
    narrow = pltpu.VMEM((tokens, LANES), f32)
    square = (heads, tokens, tokens)
    slices = pltpu.VMEM((blocks, rows, width), f32)
    flat = pltpu.VMEM((inner, width), f32)
    operands = {
        "x": xin, "z": zin, "b": bmat, "c": cmat, "ldec": ldec,
        "skip": jnp.repeat(dskip, HDIM)[None], "gain": gain[None], "w": w_out, "dout": dout,
    }
    outs = {
        "grad_x": shape((tokens, inner), bf16),
        "grad_z": shape((tokens, inner), bf16),
        "grad_b": shape((tokens, width), f32),
        "grad_c": shape((tokens, width), f32),
        "grad_w": shape(piece, f32),
        "small_total": shape((8, LANES), f32),
    }
    scratch = {
        "cum": pltpu.VMEM((heads, 1, tokens), f32), "col": pltpu.VMEM((heads, tokens, LANES), f32),
        "tail": wide, "inc": wide, "scores": pltpu.VMEM((tokens, tokens), f32),
        "decay": pltpu.VMEM(square, f32), "kern_high": pltpu.VMEM(square, bf16),
        "kern_low": pltpu.VMEM(square, bf16), "mixed": wide, "act": wide, "slope": wide, "gated": wide,
        "normed_grad": wide, "carried": wide, "grad": wide, "grad_inc": wide, "grad_values": wide,
        "normed_high": wide_half, "normed_low": wide_half, "square": narrow, "product": narrow,
        "inv": narrow, "pull": narrow, "products": pltpu.VMEM((tokens, tokens), f32),
        "part_b": narrow, "part_c": narrow,
        "state": flat, "state_grad": flat, "came_in": flat, "grad_in": flat,
        "got": slices, "before": slices, "got_grad": slices, "before_grad": slices,
        "state_sems": dma((4,)), "back_sems": dma((4,)),
        "decays": pltpu.VMEM((NX, NZ, NC, heads, 1, LANES), f32), "decay_sent": dma(()), "decay_z": dma((NZ,)),
        "decay_x": dma((NX * NC,)),
        "w_all": pltpu.VMEM((NX, NZ, NC) + piece, bf16), "w_sent": dma(()), "w_z": dma((NZ,)),
        "w_x": dma((NX,)), "w_core": dma((NX,)), "w_own": dma(()),
        "dout_all": pltpu.VMEM((groups,) + dout.shape, bf16), "d_sent": dma(()),
        "d_came": dma((2, groups // 2 + 1)),
        "dout_turned": pltpu.VMEM((groups, dout.shape[1], tokens), bf16),
        "sums": pltpu.VMEM((8, tokens), f32), "sums_got": pltpu.VMEM((groups, 8, tokens), f32),
        "sum_sems": dma((2,)),
        "small": pltpu.VMEM((8, LANES), f32), "small_got": pltpu.VMEM((blocks, 8, LANES), f32),
        "small_sems": dma((2,)),
        "grads": pltpu.VMEM((NX, NZ, NC) + piece, f32), "twin_got": pltpu.VMEM((NX, NZ) + piece, f32),
        "mid": pltpu.VMEM((NX, NZ) + piece, f32), "x_got": pltpu.VMEM((NX - 1, NZ) + piece, f32),
        "low": pltpu.VMEM((NZ,) + piece, f32), "z_got": pltpu.VMEM((NZ,) + piece, f32),
        "twin_sems": dma((2, NX)), "x_sent": dma(()), "x_came": dma((PARTS, NX)), "z_sent": dma(()),
        "z_came": dma(()),
        "got_b": pltpu.VMEM((groups, share, width), f32), "sum_b": pltpu.VMEM((share, width), f32),
        "b_sems": dma((4,)),
        "got_c": pltpu.VMEM((groups, share, width), f32), "sum_c": pltpu.VMEM((share, width), f32),
        "c_sems": dma((4,)),
    }
    names = tuple(operands) + tuple(outs) + tuple(scratch)
    vmem = pl.BlockSpec(memory_space=pltpu.VMEM)
    grad_x, grad_z, grad_b, grad_c, grad_w, small = pl.pallas_call(
        lambda *refs: whole_kernel(names, *refs),
        out_shape=tuple(outs.values()),
        in_specs=[vmem] * len(operands),
        out_specs=(vmem,) * len(outs),
        scratch_shapes=list(scratch.values()),
        name="whole",
        compiler_params=pltpu.CompilerParams(
            collective_id=0, has_side_effects=True, vmem_limit_bytes=VMEM_LIMIT
        ),
    )(*operands.values())
    pairs = heads // 2
    grad_gain = small[:pairs].reshape(-1)
    grad_skip = jnp.sum(small[pairs : 2 * pairs].reshape(heads, HDIM), axis=1)
    return grad_x, grad_z, grad_b, grad_c, grad_w, grad_gain, grad_skip


def solution(mesh):
    return jax.shard_map(
        per_device,
        mesh=mesh,
        in_specs=(
            P("ctx", "head"), P("ctx", "head"), P("ctx", None), P("ctx", None), P("head", "ctx"),
            P("head"), P("head"), P("ctx", "head"), P("ctx", "head"),
        ),
        out_specs=(
            P("ctx", "head"), P("ctx", "head"), P("ctx", None), P("ctx", None), P("ctx", "head"),
            P("head"), P("head"),
        ),
        check_vma=False,
    )
```

time: 622 us -> 115 us (0.18); the launches traced: 613 us -> 115 us
  blocking collectives: 289 us -> 0 us
  other arithmetic: 136 us -> 0.63 us
  waiting for transfers between devices: 120 us -> 0 us
  Pallas kernels: 0 us -> 106 us
  matrix products: 21 us -> 0 us
  local copies, waits for them, and re-layouts: 27.5 us -> 7.93 us
  between operations: 15 us -> 0.65 us
    psum x3 -> x0, blocking collectives: 157 us -> none  [the longest x1 129 us: per_device(): grad_gain, grad_skip = lax.psum((gain_part, skip_part), 'ctx')]
    select_n x126 -> x0, other arithmetic: 133 us -> none  [turn(): jnp.where(position < mine, new, old)]
    unnamed x1 -> x0, blocking collectives: 132 us -> none
    pallas_call x0 -> x1, Pallas kernels: none -> 106 us  [per_device(): pl.pallas_call(lambda *refs: whole_kernel(names, *refs), out_shape=tuple(...]
    psum x1 -> x0, waiting for transfers between devices: 78.6 us -> none  [per_device(): grad_b, grad_c = lax.psum((grad_b, grad_c), 'head')]
    unnamed x7 -> x0, waiting for transfers between devices: 25.9 us -> none
    dot_general x14 -> x0, matrix products: 21 us -> none  [the longest x1 5.12 us: per_device(): lax.dot_general(columns, normed, (((0,), (0,)), ((), ())), precision=HIGH...]
    all_gather x4 -> x0, waiting for transfers between devices: 15.4 us -> none  [the longest x1 15.3 us: per_device(): lax.all_gather(w_out, 'ctx', axis=0, tiled=True)]
  transfers between devices with their start and end apart: 6 -> 0, of which waited for: 3 -> 0; matrix products, arithmetic and copies ran while one was open for 28% -> 0% of each run, Pallas kernels for 0% -> 0%
where the time goes in v2:
time: 115 us
  Pallas kernels  106 us (92%)
  local copies, waits for them, and re-layouts  7.93 us (7%)
    pallas_call x1, Pallas kernels, per_device(): pl.pallas_call(lambda *refs: whole_kernel(names, *refs), out_shape=tuple(...  106 us
    unnamed x13, local copies, waits for them, and re-layouts  5.15 us

profile of v2, /device:TPU:1, one launch (start us, length us, event | category | flops | bytes accessed | tf_op | source)
XLA Modules:
  0.0 114.8 jit_solution(3490405888144743630)
XLA Ops:
  0.6 0.7 broadcast_in_dim.6
  1.4 0.7 broadcast_in_dim_reshape.3.refs_5_
  2.0 105.6 %whole.1 = (bf16[256,512]{1,0:T(8,128)(2,1)}, bf16[256,512]{1,0:T(8,128)(2,1)}, f32[256,128]{1,0:T(8,128)}, f32[256,128]{1,0:T(8,128)}, f32[32,512]{1,0:T(8,128)}, /*index=5*/f32[8,128]{1,0:T(8,128)}) custom-call(bf16[256,512]{1,0:T(8,128)(2,1)} %refs_0_.1, bf16[256,512]{1,0:T(8,128)(2,1)} %refs_1_.1, bf16[256,128]{1,0:T(8,128)(2,1)} %refs_2_.1, ...), custom_call_target="tpu_custom_call" | custom-call | tf_op jit(solution)/shard_map/whole/pallas_call | solution.py:622
  107.6 1.3 %fusion = (f32[4,128]{1,0:T(4,128)S(1)}, f32[512]{0:T(512)}) fusion(f32[8,128]{1,0:T(8,128)} %get-tuple-element.18), kind=kLoop, calls=%fused_computation.1 | loop fusion | bytes 8192 | tf_op jit(solution)/shard_map/slice | solution.py:635
  108.9 0.1 reshape.21
  109.0 0.6 reduce_sum.9
  109.7 0.0 copy-start
  109.7 1.7 %copy.21 = bf16[256,512]{1,0:T(8,128)(2,1)} copy(bf16[256,512]{1,0:T(8,128)(2,1)} %get-tuple-element.28) | data formatting | bytes 524288
  111.4 0.0 copy-done
  111.4 0.0 copy-start.2
  111.4 0.7 copy.22
  112.1 0.3 copy-done.2
  112.4 0.0 copy-start.1
  112.4 0.7 copy.23
  113.0 0.3 copy-done.1
  113.3 0.0 copy-start.3
  113.3 0.7 copy.24
  114.0 0.2 copy-done.3
  114.2 0.6 copy.25
Async XLA Ops:
  109.7 1.7 %copy-start = (bf16[256,512]{1,0:T(8,128)(2,1)S(1)}, bf16[256,512]{1,0:T(8,128)(2,1)}, u32[]{:S(2)}) copy-start(bf16[256,512]{1,0:T(8,128)(2,1)} %get-tuple-element.29) | copy-start | bytes 786436
  111.4 1.0 copy-start.2
  112.4 1.0 copy-start.1
  113.3 0.9 copy-start.3

commit v3 on v2

--- a/solution.py
+++ b/solution.py
@@ -11,7 +11,7 @@
 EPSILON = 1e-05
 MESH = pl.DeviceIdType.MESH
 NX, NZ, NC = 4, 8, 2
-PARTS = 2
+PARTS = 4
 LANES = 128
 CHUNK = 16
 VMEM_LIMIT = 56 * 2**20
@@ -73,33 +73,103 @@
     lax.fori_loop(0, count, turn, 0)
 
 
-def scan_send(state, got, sent, came):
-    mine, rows = lax.axis_index("ctx"), got.shape[1]
-    others(
-        "ctx",
-        lambda peer: remote(rows_at(state, peer, rows), got.at[mine], sent, came, ctx=peer).start(),
-    )
-    local(rows_at(state, mine, rows), got.at[mine], came).start()
-
-
-def scan_turn(got, decays, before, out, sent, came, came_back, backward):
+def chip_peers(act):
     mine = lax.axis_index("ctx")
-    count, rows = got.shape[0], got.shape[1]
-    head = mine // (HDIM // rows)
-    wait_for(got, came)
-
-    def turn(step, total):
-        index = count - 1 - step if backward else step
-        before[index] = total
-        factor = decays[
-            index // (NZ * NC), lax.rem(index // NC, NZ), lax.rem(index, NC), head
-        ]
-        return factor * total + got[index]
-
-    lax.fori_loop(0, count, turn, jnp.zeros(got.shape[1:], f32), unroll=4)
-    home = rows_at(out, mine, rows)
-    others("ctx", lambda peer: remote(before.at[peer], home, sent, came_back, ctx=peer).start())
-    local(before.at[mine], home, came_back).start()
+    chips = NX * NZ
+
+    def turn(step, carry):
+        act(lax.rem(mine // NC + step, chips))
+        return carry
+
+    lax.fori_loop(1, chips, turn, 0)
+
+
+def joined(own, other, is_first):
+    return jnp.where(is_first, own, other), jnp.where(is_first, other, own)
+
+
+class Scan:
+    def __init__(self, r, name, backward):
+        self.state, self.came = getattr(r, name + "_state"), getattr(r, name + "_came")
+        self.twin, self.half = getattr(r, name + "_twin"), getattr(r, name + "_half")
+        self.got, self.before = getattr(r, name + "_got"), getattr(r, name + "_before")
+        self.entry, self.give = getattr(r, name + "_entry"), getattr(r, name + "_give")
+        self.sems, self.r, self.backward = getattr(r, name + "_sems"), r, backward
+        mine = lax.axis_index("ctx")
+        self.core, self.chip = lax.rem(mine, NC), mine // NC
+        self.first = NC - 1 if backward else 0
+        self.is_first = self.core == self.first
+        self.heads = self.half.shape[0] // HDIM
+
+    def to_twin(self):
+        rows = self.half.shape[0]
+        remote(
+            rows_at(self.state, 1 - self.core, rows), self.twin, self.sems.at[0], self.sems.at[1],
+            ctx=self.chip * NC + 1 - self.core,
+        ).start()
+
+    def send(self):
+        wait_for(self.twin, self.sems.at[1])
+        for index in range(self.heads):
+            at = pl.ds(index * HDIM, HDIM)
+            from_state = pl.ds(pl.multiple_of(self.core * self.half.shape[0] + index * HDIM, HDIM), HDIM)
+            first, second = joined(self.state[from_state], self.twin[at], self.is_first)
+            factor = self.r.pair_decays[1 - self.first, self.core * self.heads + index]
+            self.half[at] = factor * first + second
+        rows = self.got.shape[1]
+        chip_peers(
+            lambda peer: remote(
+                rows_at(self.half, peer, rows), self.got.at[self.chip], self.sems.at[2], self.sems.at[3],
+                ctx=peer * NC + self.core,
+            ).start()
+        )
+        local(rows_at(self.half, self.chip, rows), self.got.at[self.chip], self.sems.at[3]).start()
+
+    def turn(self):
+        chips, rows = self.got.shape[0], self.got.shape[1]
+        head = self.chip // (HDIM // rows)
+        wait_for(self.got, self.sems.at[3])
+
+        def step(index, total):
+            index = chips - 1 - index if self.backward else index
+            self.before[index] = total
+            return self.r.decays[index // NZ, lax.rem(index, NZ), head] * total + self.got[index]
+
+        lax.fori_loop(0, chips, step, jnp.zeros(self.got.shape[1:], f32), unroll=4)
+        home = rows_at(self.entry, self.chip, rows)
+        chip_peers(
+            lambda peer: remote(
+                self.before.at[peer], home, self.sems.at[4], self.sems.at[5], ctx=peer * NC + self.core
+            ).start()
+        )
+        local(self.before.at[self.chip], home, self.sems.at[5]).start()
+
+    def share(self):
+        wait_for(self.entry, self.sems.at[5])
+        rows = self.half.shape[0]
+        for index in range(self.heads):
+            at = pl.ds(index * HDIM, HDIM)
+            to = pl.ds(pl.multiple_of(self.core * rows + index * HDIM, HDIM), HDIM)
+            entry = self.entry[at]
+            first, _ = joined(self.state[to], self.twin[at], self.is_first)
+            factor = self.r.pair_decays[self.first, self.core * self.heads + index]
+            later = factor * entry + first
+            self.came[to] = jnp.where(self.is_first, entry, later)
+            self.give[at] = jnp.where(self.is_first, later, entry)
+        remote(
+            self.give, rows_at(self.came, self.core, rows), self.sems.at[6], self.sems.at[7],
+            ctx=self.chip * NC + 1 - self.core,
+        ).start()
+
+    def finish(self):
+        wait_for(self.give, self.sems.at[7])
+
+    def drain(self):
+        most = self.got.at[pl.ds(0, self.got.shape[0] - 1)]
+        wait_for(self.twin, self.sems.at[0])
+        wait_for(most, self.sems.at[2])
+        wait_for(most, self.sems.at[4])
+        wait_for(self.give, self.sems.at[6])
 
 
 def shared_send(part, got, sems):
@@ -133,7 +203,7 @@
 def whole_kernel(names, *refs):
     r = types.SimpleNamespace(**dict(zip(names, refs)))
     mine, row = lax.axis_index("ctx"), lax.axis_index("head")
-    count, groups = lax.axis_size("ctx"), lax.axis_size("head")
+    groups = lax.axis_size("head")
     x, z, core = mine // (NZ * NC), lax.rem(mine // NC, NZ), lax.rem(mine, NC)
     twin = ctx_of(x, z, 1 - core)
     heads, tokens = r.ldec.shape
@@ -151,14 +221,19 @@
         return pl.ds(pl.multiple_of(chunk * CHUNK, CHUNK), CHUNK)
 
     barrier = pltpu.get_barrier_semaphore()
-    for axis in ("ctx", "head"):
-        others(
-            axis,
-            lambda peer: pl.semaphore_signal(
-                barrier, inc=1, device_id={axis: peer}, device_id_type=MESH
-            ),
+
+    def greet(**where):
+        pl.semaphore_signal(barrier, inc=1, device_id=where, device_id_type=MESH)
+
+    greet(ctx=twin)
+    chip_peers(lambda peer: greet(ctx=peer * NC + core))
+    others("head", lambda peer: greet(head=peer))
+
+    r.gain[...] = r.gain_in[...].reshape(1, inner)
+    for pair in range(pairs):
+        r.skip[:, pair * LANES : (pair + 1) * LANES] = jnp.where(
+            first_head[:1], r.dskip[2 * pair], r.dskip[2 * pair + 1]
         )
-
     token_of = lax.broadcasted_iota(jnp.int32, (tokens, tokens), 0)
     other_of = lax.broadcasted_iota(jnp.int32, (tokens, tokens), 1)
     logs = dot_nt(r.ldec[...], (token_of >= other_of).astype(f32), HIGH)
@@ -167,7 +242,7 @@
         r.cum[head] = logs[head : head + 1]
         r.col[head] = jnp.broadcast_to(columns[:, head : head + 1], (tokens, LANES))
     for head in range(heads):
-        r.decays[x, z, core, head] = jnp.exp(r.col[head, tokens - 1 : tokens, :])
+        r.pair_decays[core, head] = jnp.exp(r.col[head, tokens - 1 : tokens, :])
 
     def local_states(pair):
         lanes = pair_lanes(pair)
@@ -176,17 +251,17 @@
         r.tail[:, lanes] = tail
         r.inc[:, lanes] = jnp.exp(log)
         high, low = split(jnp.transpose(r.x[:, lanes].astype(f32) * tail))
-        r.state[pl.ds(pl.multiple_of(pair * LANES, LANES), LANES)] = dot(high, r.b[...]) + dot(
+        r.fore_state[pl.ds(pl.multiple_of(pair * LANES, LANES), LANES)] = dot(high, r.b[...]) + dot(
             low, r.b[...]
         )
 
     loop(pairs, local_states)
-    pl.semaphore_wait(barrier, count + groups - 2)
-
-    scan_send(r.state, r.got, r.state_sems.at[0], r.state_sems.at[1])
-    for step in range(1, NZ):
-        peer = ctx_of(x, lax.rem(z + step, NZ), core)
-        remote(r.decays.at[x, z, core], r.decays.at[x, z, core], r.decay_sent, r.decay_z.at[step], ctx=peer).start()
+    pl.semaphore_wait(barrier, NX * NZ + groups - 1)
+
+    fore, back = Scan(r, "fore", False), Scan(r, "back", True)
+    fore.to_twin()
+    mine_decays = r.pair_decays.at[core]
+    remote(mine_decays, mine_decays, r.pair_sems.at[0], r.pair_sems.at[1], ctx=twin).start()
     w_home = local(r.w, r.w_all.at[x, z, core], r.w_own)
     w_home.start()
     for step in range(1, NZ):
@@ -263,39 +338,40 @@
             piece = r.w_all.at[x, source, core]
             remote(piece, piece, r.w_sent, r.w_x.at[turn], ctx=peer).start()
 
+    wait_for(r.pair_decays.at[1 - core], r.pair_sems.at[1])
+    for index in range(heads // NC):
+        head = core * (heads // NC) + index
+        r.decays[x, z, index] = r.pair_decays[0, head] * r.pair_decays[1, head]
+    for step in range(1, NZ):
+        peer = ctx_of(x, lax.rem(z + step, NZ), core)
+        remote(r.decays.at[x, z], r.decays.at[x, z], r.decay_sent, r.decay_z.at[step], ctx=peer).start()
+    fore.send()
     loop(pairs // 2, inside)
-    spot = x * NC + core
-    for step in range(1, NZ):
-        wait_for(r.decays.at[x, lax.rem(z + NZ - step, NZ), core], r.decay_z.at[step])
-    for step in range(1, NX * NC):
-        other = lax.rem(spot + step, NX * NC)
-        line = r.decays.at[x, :, core]
-        remote(
-            line, line, r.decay_sent, r.decay_x.at[step], ctx=ctx_of(other // NC, z, lax.rem(other, NC))
-        ).start()
+    if far > 1:
+        ring(1)
     for step in range(1, NZ):
         relay(step)
-        if step % 2 == 0:
-            ring(step // 2)
+    if far > 2:
+        ring(2)
     w_home.wait()
     mine_line = r.w_all.at[x, :, core]
     remote(mine_line, mine_line, r.w_sent, r.w_core.at[0], ctx=twin).start()
-    for step in range(1, NX * NC):
-        other = lax.rem(spot + NX * NC - step, NX * NC)
-        wait_for(r.decays.at[other // NC, :, lax.rem(other, NC)], r.decay_x.at[step])
-    scan_turn(
-        r.got, r.decays, r.before, r.came_in, r.state_sems.at[2], r.state_sems.at[1], r.state_sems.at[3],
-        False,
-    )
-    for step in range(1, far):
-        if step > (NZ - 1) // 2:
-            ring(step)
+    for step in range(1, NZ):
+        wait_for(r.decays.at[x, lax.rem(z + NZ - step, NZ)], r.decay_z.at[step])
+    for step in range(1, NX):
+        line = r.decays.at[x]
+        remote(line, line, r.decay_sent, r.decay_x.at[step], ctx=ctx_of(lax.rem(x + step, NX), z, core)).start()
+    for step in range(1, NX):
+        wait_for(r.decays.at[lax.rem(x + NX - step, NX)], r.decay_x.at[step])
+    fore.turn()
+    lax.fori_loop(pairs // 2, pairs, lambda pair, carry: (inside(pair), carry)[1], 0)
+    for step in range(3, far):
+        ring(step)
+    loop(chunks, gate)
     for turn in range(NX - 1):
         line = r.w_all.at[lax.rem(x + NX - turn - 1, NX), :, core]
         wait_for(line, r.w_x.at[turn])
         remote(line, line, r.w_sent, r.w_core.at[turn + 1], ctx=twin).start()
-    lax.fori_loop(pairs // 2, pairs, lambda pair, carry: (inside(pair), carry)[1], 0)
-    loop(chunks, gate)
     r.dout_all[row] = r.dout[...]
     wait_for(r.dout_all.at[lax.rem(row + groups - far, groups)], r.d_came.at[0, far])
     if near:
@@ -305,29 +381,19 @@
         r.dout_turned[piece] = jnp.transpose(r.dout_all[piece])
 
     loop(groups, turned)
+    piece_rows, piece_width = r.w.shape[0], r.dout.shape[1]
+    line_pieces = NZ * NC * piece_rows // piece_width
+
     for turn in range(NX):
         wait_for(r.w_all.at[lax.rem(x + NX - turn, NX), :, 1 - core], r.w_core.at[turn])
-    piece_rows, piece_width = r.w.shape[0], r.dout.shape[1]
-    deep = piece_width // (piece_rows * NC)
-    line_pieces = NZ // deep
-
-    def project(piece):
-        z_from = pl.ds(lax.rem(piece, line_pieces) * deep, deep)
-        block = r.w_all[piece // line_pieces, z_from].reshape(piece_width, inner)
-        value = dot(r.dout_all[piece], block)
-
-        @pl.when(piece == 0)
-        def _():
-            r.normed_grad[...] = value
-
-        @pl.when(piece > 0)
-        def _():
-            r.normed_grad[...] += value
-
-    loop(groups, project)
-
-    wait_for(r.came_in, r.state_sems.at[3])
-    in_high, in_low = split(r.came_in[...])
+    r.normed_grad[...] = dot(
+        jnp.concatenate([r.dout_all[piece] for piece in range(groups)], axis=1),
+        r.w_all[...].reshape(groups * piece_width, inner),
+    )
+
+    fore.share()
+    fore.finish()
+    in_high, in_low = split(r.fore_came[...])
     r.carried[...] = dot_nt(r.c[...], in_high) + dot_nt(r.c[...], in_low)
 
     def gated_rows(chunk):
@@ -336,37 +402,40 @@
         gated = mixed * r.act[at, :]
         r.mixed[at, :] = mixed
         r.gated[at, :] = gated
-        square = gated * gated
-        product = r.gain[...] * r.normed_grad[at, :] * gated
-        fold = lambda value: sum(
-            value[:, lane : lane + LANES] for lane in range(LANES, inner, LANES)
-        ) + value[:, :LANES]
-        r.square[at, :] = fold(square)
-        r.product[at, :] = fold(product)
+        r.square[at, :] = lane_fold(gated * gated)
+        r.product[at, :] = lane_fold(r.gain[...] * r.normed_grad[at, :] * gated)
+
+    def lane_fold(value):
+        return sum(value[:, lane : lane + LANES] for lane in range(LANES, inner, LANES)) + value[:, :LANES]
+
+    ones = jnp.ones((8, LANES), f32)
+
+    def wide(value):
+        return jnp.concatenate([value] * (inner // LANES), axis=1)
 
     loop(chunks, gated_rows)
-    ones = jnp.ones((8, LANES), f32)
     top_row = lax.broadcasted_iota(jnp.int32, (8, tokens), 0) == 0
     r.sums[...] = jnp.where(
         top_row, dot_nt(ones, r.square[...], HIGH), dot_nt(ones, r.product[...], HIGH)
     )
     others(
-        "head", lambda peer: remote(r.sums, r.sums_got.at[row], r.sum_sems.at[0], r.sum_sems.at[1], head=peer).start()
+        "head",
+        lambda peer: remote(r.sums, r.sums_got.at[row], r.sum_sems.at[0], r.sum_sems.at[1], head=peer).start(),
     )
     local(r.sums, r.sums_got.at[row], r.sum_sems.at[1]).start()
     wait_for(r.sums_got, r.sum_sems.at[1])
     total = r.sums_got[0]
     for index in range(1, groups):
         total = total + r.sums_got[index]
-    inv = lax.rsqrt(total[0:1] / features + EPSILON)
-    pull = inv * inv * inv * (total[1:2] / features)
+    total = total / features
+    inv = lax.rsqrt(total[0:1] + EPSILON)
+    pull = inv * inv * inv * total[1:2]
     both = jnp.transpose(jnp.where(top_row, inv, pull))
     r.inv[...] = jnp.broadcast_to(both[:, 0:1], (tokens, LANES))
     r.pull[...] = jnp.broadcast_to(both[:, 1:2], (tokens, LANES))
 
     def gradient_rows(chunk, sums):
         at = chunk_rows(chunk)
-        wide = lambda value: jnp.concatenate([value] * (inner // LANES), axis=1)
         inv, pull = wide(r.inv[at, :]), wide(r.pull[at, :])
         gated, normed_grad = r.gated[at, :], r.normed_grad[at, :]
         scaled = gated * inv
@@ -390,19 +459,15 @@
         r.small[index : index + 1, :] = gain_sum[:, lanes]
         r.small[pairs + index : pairs + index + 1, :] = skip_sum[:, lanes]
 
-    all_but_one = r.got.at[pl.ds(0, count - 1)]
-    wait_for(all_but_one, r.state_sems.at[0])
-    wait_for(all_but_one, r.state_sems.at[2])
-
     def local_gradients(pair):
         lanes = pair_lanes(pair)
         high, low = split(jnp.transpose(r.grad_inc[:, lanes]))
-        r.state_grad[pl.ds(pl.multiple_of(pair * LANES, LANES), LANES)] = dot(high, r.c[...]) + dot(
+        r.back_state[pl.ds(pl.multiple_of(pair * LANES, LANES), LANES)] = dot(high, r.c[...]) + dot(
             low, r.c[...]
         )
 
     loop(pairs, local_gradients)
-    scan_send(r.state_grad, r.got_grad, r.back_sems.at[0], r.back_sems.at[1])
+    back.to_twin()
 
     order = [lax.rem(x + step, NX) for step in range(1, NX + 1)]
     depth = NZ // PARTS
@@ -416,27 +481,14 @@
             r.grads.at[order[step], :, 1 - core], r.twin_got.at[order[step]], r.twin_sems.at[0, step],
             r.twin_sems.at[1, step], ctx=twin,
         ).start()
-    others(
-        "ctx", lambda peer: remote(r.small, r.small_got.at[mine], r.small_sems.at[0], r.small_sems.at[1], ctx=peer).start()
-    )
-    local(r.small, r.small_got.at[mine], r.small_sems.at[1]).start()
-    for step in range(NX):
-        wait_for(r.twin_got.at[order[step]], r.twin_sems.at[1, step])
-
-        def add(index):
-            r.mid[order[step], index] = (
-                r.grads[order[step], index, core] + r.twin_got[order[step], index]
-            )
-
-        loop(NZ, add)
-        if step < NX - 1:
-            for part in range(PARTS):
-                block = pl.ds(part * depth, depth)
-                remote(
-                    r.mid.at[order[step], block], r.x_got.at[step, block], r.x_sent,
-                    r.x_came.at[part, step], ctx=ctx_of(order[step], z, core),
-                ).start()
-
+
+    remote(r.small, r.small_twin, r.small_sems.at[0], r.small_sems.at[1], ctx=twin).start()
+    back.send()
+    wait_for(r.small_twin, r.small_sems.at[1])
+    r.small_z[z] = r.small[...] + r.small_twin[...]
+    for step in range(1, NZ):
+        peer = ctx_of(x, lax.rem(z + step, NZ), core)
+        remote(r.small_z.at[z], r.small_z.at[z], r.small_sems.at[2], r.small_sems.at[3], ctx=peer).start()
     def products(pair):
         lanes = pair_lanes(pair)
         grad = r.grad[:, lanes]
@@ -469,8 +521,27 @@
 
     r.products[...] = jnp.zeros_like(r.products)
     loop(pairs, products)
+    for step in range(NX):
+        wait_for(r.twin_got.at[order[step]], r.twin_sems.at[1, step])
+
+        def add(index):
+            r.mid[order[step], index] = (
+                r.grads[order[step], index, core] + r.twin_got[order[step], index]
+            )
+
+        loop(NZ, add)
+
+    def along_x(part):
+        for step in range(NX - 1):
+            block = pl.ds(part * depth, depth)
+            remote(
+                r.mid.at[order[step], block], r.x_got.at[step, block], r.x_sent,
+                r.x_came.at[part, step], ctx=ctx_of(order[step], z, core),
+            ).start()
+
+    along_x(0)
     high, low = split(r.products[...])
-    in_high, in_low = split(r.came_in[...])
+    in_high, in_low = split(r.fore_came[...])
     out_high, out_low = split(r.grad_inc[...])
     r.part_c[...] = (
         dot(high, r.b[...]) + dot(low, r.b[...])
@@ -479,12 +550,6 @@
     shared_send(r.part_c, r.got_c, r.c_sems)
     high, low = split(jnp.transpose(r.products[...]))
     r.part_b[...] = dot(high, r.c[...]) + dot(low, r.c[...])
-
-    scan_turn(
-        r.got_grad, r.decays, r.before_grad, r.grad_in, r.back_sems.at[2], r.back_sems.at[1],
-        r.back_sems.at[3], True,
-    )
-    shared_turn(r.got_c, r.sum_c, r.grad_c, r.c_sems)
 
     def fold_part(part):
         block = pl.ds(part * depth, depth)
@@ -509,9 +574,23 @@
 
         loop(NZ, fold)
 
+    back.turn()
+    for part in range(1, PARTS):
+        along_x(part)
+    shared_turn(r.got_c, r.sum_c, r.grad_c, r.c_sems)
+
     fold_part(0)
-    wait_for(r.grad_in, r.back_sems.at[3])
-    in_high, in_low = split(r.grad_in[...])
+    back.share()
+    wait_for(r.small_z.at[pl.ds(0, NZ - 1)], r.small_sems.at[3])
+    value = r.small_z[0]
+    for index in range(1, NZ):
+        value = value + r.small_z[index]
+    r.small_x[x] = value
+    for step in range(1, NX):
+        peer = ctx_of(lax.rem(x + step, NX), z, core)
+        remote(r.small_x.at[x], r.small_x.at[x], r.small_sems.at[4], r.small_sems.at[5], ctx=peer).start()
+    back.finish()
+    in_high, in_low = split(r.back_came[...])
     r.carried[...] = dot_nt(r.b[...], in_high) + dot_nt(r.b[...], in_low)
 
     def weigh(chunk):
@@ -526,12 +605,14 @@
     shared_send(r.part_b, r.got_b, r.b_sems)
     for part in range(1, PARTS):
         fold_part(part)
+        if part == PARTS // 2:
+            shared_turn(r.got_b, r.sum_b, r.grad_b, r.b_sems)
     local(r.low.at[z], r.z_got.at[z], r.z_came).start()
-    shared_turn(r.got_b, r.sum_b, r.grad_b, r.b_sems)
-    wait_for(r.small_got, r.small_sems.at[1])
-    r.small_total[...] = lax.fori_loop(
-        1, count, lambda index, value: value + r.small_got[index], r.small_got[0]
-    )
+    wait_for(r.small_x.at[pl.ds(0, NX - 1)], r.small_sems.at[5])
+    value = r.small_x[0]
+    for index in range(1, NX):
+        value = value + r.small_x[index]
+    r.small_total[...] = value
     wait_for(r.z_got, r.z_came)
     value = r.z_got[0]
     for index in range(1, NZ):
@@ -540,9 +621,12 @@
 
     shared_end(r.got_c, r.grad_c, r.c_sems)
     shared_end(r.got_b, r.grad_b, r.b_sems)
-    wait_for(all_but_one, r.back_sems.at[0])
-    wait_for(all_but_one, r.back_sems.at[2])
-    wait_for(r.small_got.at[pl.ds(0, count - 1)], r.small_sems.at[0])
+    fore.drain()
+    back.drain()
+    wait_for(r.pair_decays.at[core], r.pair_sems.at[0])
+    wait_for(r.small, r.small_sems.at[0])
+    wait_for(r.small_z.at[pl.ds(0, NZ - 1)], r.small_sems.at[2])
+    wait_for(r.small_x.at[pl.ds(0, NX - 1)], r.small_sems.at[4])
     for step in range(NX):
         wait_for(r.twin_got.at[step], r.twin_sems.at[0, step])
     for step in range(NX - 1):
@@ -550,12 +634,25 @@
     wait_for(r.z_got.at[pl.ds(0, NZ - 1)], r.z_sent)
     wait_for(r.dout_all.at[pl.ds(0, groups - 1)], r.d_sent)
     wait_for(r.sums_got.at[pl.ds(0, groups - 1)], r.sum_sems.at[0])
-    wait_for(r.decays.at[0, pl.ds(0, NZ - 1), 0], r.decay_sent)
-    for step in range(1, NX * NC):
-        wait_for(r.decays.at[0, :, 0], r.decay_sent)
+    wait_for(r.decays.at[0, pl.ds(0, NZ - 1)], r.decay_sent)
+    wait_for(r.decays.at[pl.ds(0, NX - 1)], r.decay_sent)
     for turn in range(2 * NX - 1):
         wait_for(r.w_all.at[turn % NX, :, 0], r.w_sent)
     wait_for(r.w_all.at[0, pl.ds(0, NZ - 1), 0], r.w_sent)
+
+
+def leave_kernel(*refs):
+    made, small, outs, gain, skip, sems = refs[:5], refs[5], refs[6:11], refs[11], refs[12], refs[13]
+    for index in range(5):
+        local(made[index], outs[index], sems.at[index]).start()
+    pairs = skip.shape[0] // 2
+    for pair in range(pairs):
+        gain[pl.ds(pair * LANES, LANES)] = small[pair]
+        line = small[pairs + pair : pairs + pair + 1]
+        for side in (0, 1):
+            skip[2 * pair + side] = jnp.sum(line[:, side * HDIM : (side + 1) * HDIM])
+    for index in range(5):
+        local(made[index], outs[index], sems.at[index]).wait()
 
 
 def per_device(xin, zin, bmat, cmat, ldec, dskip, gain, w_out, dout):
@@ -570,11 +667,12 @@
     wide_half = pltpu.VMEM((tokens, inner), bf16)
     narrow = pltpu.VMEM((tokens, LANES), f32)
     square = (heads, tokens, tokens)
-    slices = pltpu.VMEM((blocks, rows, width), f32)
+    slices = pltpu.VMEM((blocks // NC, rows, width), f32)
+    half_flat = pltpu.VMEM((inner // NC, width), f32)
     flat = pltpu.VMEM((inner, width), f32)
     operands = {
         "x": xin, "z": zin, "b": bmat, "c": cmat, "ldec": ldec,
-        "skip": jnp.repeat(dskip, HDIM)[None], "gain": gain[None], "w": w_out, "dout": dout,
+        "dskip": dskip, "gain_in": gain, "w": w_out, "dout": dout,
     }
     outs = {
         "grad_x": shape((tokens, inner), bf16),
@@ -585,6 +683,7 @@
         "small_total": shape((8, LANES), f32),
     }
     scratch = {
+        "skip": pltpu.VMEM((1, inner), f32), "gain": pltpu.VMEM((1, inner), f32),
         "cum": pltpu.VMEM((heads, 1, tokens), f32), "col": pltpu.VMEM((heads, tokens, LANES), f32),
         "tail": wide, "inc": wide, "scores": pltpu.VMEM((tokens, tokens), f32),
         "decay": pltpu.VMEM(square, f32), "kern_high": pltpu.VMEM(square, bf16),
@@ -593,11 +692,12 @@
         "normed_high": wide_half, "normed_low": wide_half, "square": narrow, "product": narrow,
         "inv": narrow, "pull": narrow, "products": pltpu.VMEM((tokens, tokens), f32),
         "part_b": narrow, "part_c": narrow,
-        "state": flat, "state_grad": flat, "came_in": flat, "grad_in": flat,
-        "got": slices, "before": slices, "got_grad": slices, "before_grad": slices,
-        "state_sems": dma((4,)), "back_sems": dma((4,)),
-        "decays": pltpu.VMEM((NX, NZ, NC, heads, 1, LANES), f32), "decay_sent": dma(()), "decay_z": dma((NZ,)),
-        "decay_x": dma((NX * NC,)),
+        "pair_decays": pltpu.VMEM((NC, heads, 1, LANES), f32), "pair_sems": dma((2,)),
+        "decays": pltpu.VMEM((NX, NZ, heads // NC, 1, LANES), f32), "decay_sent": dma(()),
+        "decay_z": dma((NZ,)), "decay_x": dma((NX,)),
+        "small": pltpu.VMEM((8, LANES), f32), "small_twin": pltpu.VMEM((8, LANES), f32),
+        "small_z": pltpu.VMEM((NZ, 8, LANES), f32), "small_x": pltpu.VMEM((NX, 8, LANES), f32),
+        "small_sems": dma((6,)),
         "w_all": pltpu.VMEM((NX, NZ, NC) + piece, bf16), "w_sent": dma(()), "w_z": dma((NZ,)),
         "w_x": dma((NX,)), "w_core": dma((NX,)), "w_own": dma(()),
         "dout_all": pltpu.VMEM((groups,) + dout.shape, bf16), "d_sent": dma(()),
@@ -605,8 +705,6 @@
         "dout_turned": pltpu.VMEM((groups, dout.shape[1], tokens), bf16),
         "sums": pltpu.VMEM((8, tokens), f32), "sums_got": pltpu.VMEM((groups, 8, tokens), f32),
         "sum_sems": dma((2,)),
-        "small": pltpu.VMEM((8, LANES), f32), "small_got": pltpu.VMEM((blocks, 8, LANES), f32),
-        "small_sems": dma((2,)),
         "grads": pltpu.VMEM((NX, NZ, NC) + piece, f32), "twin_got": pltpu.VMEM((NX, NZ) + piece, f32),
         "mid": pltpu.VMEM((NX, NZ) + piece, f32), "x_got": pltpu.VMEM((NX - 1, NZ) + piece, f32),
         "low": pltpu.VMEM((NZ,) + piece, f32), "z_got": pltpu.VMEM((NZ,) + piece, f32),
@@ -617,12 +715,18 @@
         "got_c": pltpu.VMEM((groups, share, width), f32), "sum_c": pltpu.VMEM((share, width), f32),
         "c_sems": dma((4,)),
     }
+    for name in ("fore", "back"):
+        scratch |= {
+            name + "_state": flat, name + "_came": flat, name + "_twin": half_flat, name + "_half": half_flat,
+            name + "_got": slices, name + "_before": slices, name + "_entry": half_flat,
+            name + "_give": half_flat, name + "_sems": dma((8,)),
+        }
     names = tuple(operands) + tuple(outs) + tuple(scratch)
     vmem = pl.BlockSpec(memory_space=pltpu.VMEM)
-    grad_x, grad_z, grad_b, grad_c, grad_w, small = pl.pallas_call(
+    made = pl.pallas_call(
         lambda *refs: whole_kernel(names, *refs),
         out_shape=tuple(outs.values()),
-        in_specs=[vmem] * len(operands),
+        in_specs=[pl.BlockSpec(memory_space=pltpu.SMEM) if key == "dskip" else vmem for key in operands],
         out_specs=(vmem,) * len(outs),
         scratch_shapes=list(scratch.values()),
         name="whole",
@@ -630,10 +734,16 @@
             collective_id=0, has_side_effects=True, vmem_limit_bytes=VMEM_LIMIT
         ),
     )(*operands.values())
-    pairs = heads // 2
-    grad_gain = small[:pairs].reshape(-1)
-    grad_skip = jnp.sum(small[pairs : 2 * pairs].reshape(heads, HDIM), axis=1)
-    return grad_x, grad_z, grad_b, grad_c, grad_w, grad_gain, grad_skip
+    anywhere = pl.BlockSpec(memory_space=pl.ANY)
+    whole = tuple(outs.values())[:5]
+    return pl.pallas_call(
+        leave_kernel,
+        out_shape=whole + (shape((inner,), f32), shape((heads,), f32)),
+        in_specs=[vmem] * 6,
+        out_specs=(anywhere,) * 5 + (vmem, pl.BlockSpec(memory_space=pltpu.SMEM)),
+        scratch_shapes=[dma((5,))],
+        name="leave",
+    )(*made)
 
 
 def solution(mesh):

time: 115 us -> 96.9 us (0.84)
  Pallas kernels: 106 us -> 96.1 us
  local copies, waits for them, and re-layouts: 7.93 us -> 0 us
    pallas_call x1, Pallas kernels: 106 us -> 93.5 us  [per_device(): pl.pallas_call(lambda *refs: whole_kernel(names, *refs), out_shape=tuple(...]
    unnamed x13 -> x0, local copies, waits for them, and re-layouts: 5.15 us -> none
    pallas_call x0 -> x1, Pallas kernels: none -> 2.65 us  [per_device(): pl.pallas_call(leave_kernel, out_shape=whole + (shape((inner,), f32), sha...]
    slice x1 -> x0, local copies, waits for them, and re-layouts: 1.33 us -> none  [per_device(): grad_skip = jnp.sum(small[pairs:2 * pairs].reshape(heads, HDIM), axis=1)]
where the time goes in v3:
time: 96.9 us; the launch traced here: 96.8 us
  Pallas kernels  96.1 us (99%)
    pallas_call x1, Pallas kernels, per_device(): pl.pallas_call(lambda *refs: whole_kernel(names, *refs), out_shape=tuple(...  93.5 us
    pallas_call x1, Pallas kernels, per_device(): pl.pallas_call(leave_kernel, out_shape=whole + (shape((inner,), f32), sha...  2.65 us

profile of v3, /device:TPU:1, one launch (start us, length us, event | category | flops | bytes accessed | tf_op | source)
XLA Modules:
  0.0 96.8 jit_solution(18145434571465299351)
XLA Ops:
  0.6 93.5 %whole.1 = (bf16[256,512]{1,0:T(8,128)(2,1)}, bf16[256,512]{1,0:T(8,128)(2,1)}, f32[256,128]{1,0:T(8,128)}, f32[256,128]{1,0:T(8,128)}, f32[32,512]{1,0:T(8,128)}, /*index=5*/f32[8,128]{1,0:T(8,128)}) custom-call(bf16[256,512]{1,0:T(8,128)(2,1)} %refs_0_.1, bf16[256,512]{1,0:T(8,128)(2,1)} %refs_1_.1, bf16[256,128]{1,0:T(8,128)(2,1)} %refs_2_.1, ...), custom_call_target="tpu_custom_call" | custom-call | tf_op jit(solution)/shard_map/whole/pallas_call | solution.py:726
  94.1 2.6 %leave.1 = (bf16[256,512]{1,0:T(8,128)(2,1)}, bf16[256,512]{1,0:T(8,128)(2,1)}, f32[256,128]{1,0:T(8,128)}, f32[256,128]{1,0:T(8,128)}, f32[32,512]{1,0:T(8,128)}, /*index=5*/f32[512]{0:T(512)}, f32[8]{0:T(128)}) custom-call(bf16[256,512]{1,0:T(8,128)(2,1)} %get-tuple-element.13.refs_0_, bf16[256,512]{1,0:T(8,128)(2,1)} %get-tuple-element.14.refs_1_, ...), custom_call_target="tpu_custom_call" | custom-call | tf_op jit(solution)/shard_map/leave/pallas_call | solution.py:739

commit v4 on v3

--- a/solution.py
+++ b/solution.py
@@ -469,7 +469,8 @@
     loop(pairs, local_gradients)
     back.to_twin()
 
-    order = [lax.rem(x + step, NX) for step in range(1, NX + 1)]
+    ahead, across, behind = [lax.rem(x + step, NX) for step in range(1, NX)]
+    order = [across, ahead, behind, x]
     depth = NZ // PARTS
     for step in range(NX):
         left_side = jnp.concatenate(
@@ -489,6 +490,25 @@
     for step in range(1, NZ):
         peer = ctx_of(x, lax.rem(z + step, NZ), core)
         remote(r.small_z.at[z], r.small_z.at[z], r.small_sems.at[2], r.small_sems.at[3], ctx=peer).start()
+    def add_twin(step):
+        wait_for(r.twin_got.at[order[step]], r.twin_sems.at[1, step])
+
+        def add(index):
+            r.mid[order[step], index] = (
+                r.grads[order[step], index, core] + r.twin_got[order[step], index]
+            )
+
+        loop(NZ, add)
+
+    add_twin(0)
+    via = NZ // 2
+    sides = ((0, ahead), (1, behind))
+    for side, target in sides:
+        remote(
+            r.mid.at[across, pl.ds(side * via, via)], r.passing.at[side], r.pass_sems.at[0, side],
+            r.pass_sems.at[1, side], ctx=ctx_of(target, z, core),
+        ).start()
+
     def products(pair):
         lanes = pair_lanes(pair)
         grad = r.grad[:, lanes]
@@ -521,25 +541,26 @@
 
     r.products[...] = jnp.zeros_like(r.products)
     loop(pairs, products)
-    for step in range(NX):
-        wait_for(r.twin_got.at[order[step]], r.twin_sems.at[1, step])
-
-        def add(index):
-            r.mid[order[step], index] = (
-                r.grads[order[step], index, core] + r.twin_got[order[step], index]
-            )
-
-        loop(NZ, add)
+    for step in range(1, NX):
+        add_twin(step)
+
+    def pass_on():
+        for side, target in sides:
+            wait_for(r.passing.at[side], r.pass_sems.at[1, side])
+
+            def join(index):
+                r.mid[target, side * via + index] += r.passing[side, index]
+
+            loop(via, join)
 
     def along_x(part):
-        for step in range(NX - 1):
-            block = pl.ds(part * depth, depth)
+        block = pl.ds(part * depth, depth)
+        for side, target in sides:
             remote(
-                r.mid.at[order[step], block], r.x_got.at[step, block], r.x_sent,
-                r.x_came.at[part, step], ctx=ctx_of(order[step], z, core),
+                r.mid.at[target, block], r.x_got.at[side, block], r.x_sent, r.x_came.at[part, side],
+                ctx=ctx_of(target, z, core),
             ).start()
 
-    along_x(0)
     high, low = split(r.products[...])
     in_high, in_low = split(r.fore_came[...])
     out_high, out_low = split(r.grad_inc[...])
@@ -553,18 +574,15 @@
 
     def fold_part(part):
         block = pl.ds(part * depth, depth)
-        for step in range(NX - 1):
-            wait_for(r.x_got.at[step, block], r.x_came.at[part, step])
+        for side in (0, 1):
+            wait_for(r.x_got.at[side, block], r.x_came.at[part, side])
 
         def fold(turn):
             index = lax.rem(z + turn + 1, NZ)
 
             @pl.when((index >= part * depth) & (index < (part + 1) * depth))
             def _():
-                value = r.mid[x, index]
-                for step in range(NX - 1):
-                    value = value + r.x_got[step, index]
-                r.low[index] = value
+                r.low[index] = r.mid[x, index] + r.x_got[0, index] + r.x_got[1, index]
 
                 @pl.when(index != z)
                 def _():
@@ -575,7 +593,8 @@
         loop(NZ, fold)
 
     back.turn()
-    for part in range(1, PARTS):
+    pass_on()
+    for part in range(PARTS):
         along_x(part)
     shared_turn(r.got_c, r.sum_c, r.grad_c, r.c_sems)
 
@@ -605,7 +624,7 @@
     shared_send(r.part_b, r.got_b, r.b_sems)
     for part in range(1, PARTS):
         fold_part(part)
-        if part == PARTS // 2:
+        if part == PARTS - 1:
             shared_turn(r.got_b, r.sum_b, r.grad_b, r.b_sems)
     local(r.low.at[z], r.z_got.at[z], r.z_came).start()
     wait_for(r.small_x.at[pl.ds(0, NX - 1)], r.small_sems.at[5])
@@ -629,8 +648,9 @@
     wait_for(r.small_x.at[pl.ds(0, NX - 1)], r.small_sems.at[4])
     for step in range(NX):
         wait_for(r.twin_got.at[step], r.twin_sems.at[0, step])
-    for step in range(NX - 1):
-        wait_for(r.x_got.at[step], r.x_sent)
+    for side in (0, 1):
+        wait_for(r.x_got.at[side], r.x_sent)
+        wait_for(r.passing.at[side], r.pass_sems.at[0, side])
     wait_for(r.z_got.at[pl.ds(0, NZ - 1)], r.z_sent)
     wait_for(r.dout_all.at[pl.ds(0, groups - 1)], r.d_sent)
     wait_for(r.sums_got.at[pl.ds(0, groups - 1)], r.sum_sems.at[0])
@@ -706,7 +726,8 @@
         "sums": pltpu.VMEM((8, tokens), f32), "sums_got": pltpu.VMEM((groups, 8, tokens), f32),
         "sum_sems": dma((2,)),
         "grads": pltpu.VMEM((NX, NZ, NC) + piece, f32), "twin_got": pltpu.VMEM((NX, NZ) + piece, f32),
-        "mid": pltpu.VMEM((NX, NZ) + piece, f32), "x_got": pltpu.VMEM((NX - 1, NZ) + piece, f32),
+        "mid": pltpu.VMEM((NX, NZ) + piece, f32), "x_got": pltpu.VMEM((2, NZ) + piece, f32), "passing": pltpu.VMEM((2, NZ // 2) + piece, f32),
+        "pass_sems": dma((2, 2)),
         "low": pltpu.VMEM((NZ,) + piece, f32), "z_got": pltpu.VMEM((NZ,) + piece, f32),
         "twin_sems": dma((2, NX)), "x_sent": dma(()), "x_came": dma((PARTS, NX)), "z_sent": dma(()),
         "z_came": dma(()),

time: 96.9 us -> 90.7 us (0.936)
  Pallas kernels: 96.1 us -> 89.9 us
    pallas_call x1, Pallas kernels: 93.5 us -> 87.3 us  [per_device(): pl.pallas_call(lambda *refs: whole_kernel(names, *refs), out_shape=tuple(...]
where the time goes in v4:
time: 90.7 us; the launch traced here: 90.6 us
  Pallas kernels  89.9 us (99%)
    pallas_call x1, Pallas kernels, per_device(): pl.pallas_call(lambda *refs: whole_kernel(names, *refs), out_shape=tuple(...  87.3 us
    pallas_call x1, Pallas kernels, per_device(): pl.pallas_call(leave_kernel, out_shape=whole + (shape((inner,), f32), sha...  2.65 us

profile of v4, /device:TPU:1, one launch (start us, length us, event | category | flops | bytes accessed | tf_op | source)
XLA Modules:
  0.0 90.6 jit_solution(15987222974612078377)
XLA Ops:
  0.6 87.3 %whole.1 = (bf16[256,512]{1,0:T(8,128)(2,1)}, bf16[256,512]{1,0:T(8,128)(2,1)}, f32[256,128]{1,0:T(8,128)}, f32[256,128]{1,0:T(8,128)}, f32[32,512]{1,0:T(8,128)}, /*index=5*/f32[8,128]{1,0:T(8,128)}) custom-call(bf16[256,512]{1,0:T(8,128)(2,1)} %refs_0_.1, bf16[256,512]{1,0:T(8,128)(2,1)} %refs_1_.1, bf16[256,128]{1,0:T(8,128)(2,1)} %refs_2_.1, ...), custom_call_target="tpu_custom_call" | custom-call | tf_op jit(solution)/shard_map/whole/pallas_call | solution.py:747
  87.9 2.6 %leave.1 = (bf16[256,512]{1,0:T(8,128)(2,1)}, bf16[256,512]{1,0:T(8,128)(2,1)}, f32[256,128]{1,0:T(8,128)}, f32[256,128]{1,0:T(8,128)}, f32[32,512]{1,0:T(8,128)}, /*index=5*/f32[512]{0:T(512)}, f32[8]{0:T(128)}) custom-call(bf16[256,512]{1,0:T(8,128)(2,1)} %get-tuple-element.13.refs_0_, bf16[256,512]{1,0:T(8,128)(2,1)} %get-tuple-element.14.refs_1_, ...), custom_call_target="tpu_custom_call" | custom-call | tf_op jit(solution)/shard_map/leave/pallas_call | solution.py:760

commit v5 on v4

--- a/solution.py
+++ b/solution.py
@@ -598,7 +598,6 @@
         along_x(part)
     shared_turn(r.got_c, r.sum_c, r.grad_c, r.c_sems)
 
-    fold_part(0)
     back.share()
     wait_for(r.small_z.at[pl.ds(0, NZ - 1)], r.small_sems.at[3])
     value = r.small_z[0]
@@ -608,6 +607,7 @@
     for step in range(1, NX):
         peer = ctx_of(lax.rem(x + step, NX), z, core)
         remote(r.small_x.at[x], r.small_x.at[x], r.small_sems.at[4], r.small_sems.at[5], ctx=peer).start()
+    fold_part(0)
     back.finish()
     in_high, in_low = split(r.back_came[...])
     r.carried[...] = dot_nt(r.b[...], in_high) + dot_nt(r.b[...], in_low)
@@ -624,8 +624,7 @@
     shared_send(r.part_b, r.got_b, r.b_sems)
     for part in range(1, PARTS):
         fold_part(part)
-        if part == PARTS - 1:
-            shared_turn(r.got_b, r.sum_b, r.grad_b, r.b_sems)
+    shared_turn(r.got_b, r.sum_b, r.grad_b, r.b_sems)
     local(r.low.at[z], r.z_got.at[z], r.z_came).start()
     wait_for(r.small_x.at[pl.ds(0, NX - 1)], r.small_sems.at[5])
     value = r.small_x[0]

time: 90.7 us -> 90.7 us (level)
  no operation moved by 1% of the time
where the time goes in v5:
time: 90.7 us; the launch traced here: 90.6 us
  Pallas kernels  89.9 us (99%)
    pallas_call x1, Pallas kernels, per_device(): pl.pallas_call(lambda *refs: whole_kernel(names, *refs), out_shape=tuple(...  87.3 us
    pallas_call x1, Pallas kernels, per_device(): pl.pallas_call(leave_kernel, out_shape=whole + (shape((inner,), f32), sha...  2.65 us

profile of v5, /device:TPU:1, one launch (start us, length us, event | category | flops | bytes accessed | tf_op | source)
XLA Modules:
  0.0 90.6 jit_solution(8341132412215681582)
XLA Ops:
  0.6 87.3 %whole.1 = (bf16[256,512]{1,0:T(8,128)(2,1)}, bf16[256,512]{1,0:T(8,128)(2,1)}, f32[256,128]{1,0:T(8,128)}, f32[256,128]{1,0:T(8,128)}, f32[32,512]{1,0:T(8,128)}, /*index=5*/f32[8,128]{1,0:T(8,128)}) custom-call(bf16[256,512]{1,0:T(8,128)(2,1)} %refs_0_.1, bf16[256,512]{1,0:T(8,128)(2,1)} %refs_1_.1, bf16[256,128]{1,0:T(8,128)(2,1)} %refs_2_.1, ...), custom_call_target="tpu_custom_call" | custom-call | tf_op jit(solution)/shard_map/whole/pallas_call | solution.py:746
  87.9 2.6 %leave.1 = (bf16[256,512]{1,0:T(8,128)(2,1)}, bf16[256,512]{1,0:T(8,128)(2,1)}, f32[256,128]{1,0:T(8,128)}, f32[256,128]{1,0:T(8,128)}, f32[32,512]{1,0:T(8,128)}, /*index=5*/f32[512]{0:T(512)}, f32[8]{0:T(128)}) custom-call(bf16[256,512]{1,0:T(8,128)(2,1)} %get-tuple-element.13.refs_0_, bf16[256,512]{1,0:T(8,128)(2,1)} %get-tuple-element.14.refs_1_, ...), custom_call_target="tpu_custom_call" | custom-call | tf_op jit(solution)/shard_map/leave/pallas_call | solution.py:759
